TPU v7x, 256 devices: a whole 4x4x8 slice. The times are simulated.
256 devices in a mesh: row: 64 (over z, y, core), rep: 4 (over x).
Axes of the slice: x: 4, y: 4, z: 8, core: 2. Of those that a mesh axis runs over, the one named last changes fastest.
Arguments:
- params: float32 [59, 262144], P(None, 'row'), may hold values from -6 to 6, as said below
- first_moment: float32 [59, 262144], P(None, 'row'), may hold values from -6 to 6
- second_moment: float32 [59, 262144], P(None, 'row'), may hold values from 0.01 to 1
- camera: float32 [2, 4, 11], P(None, 'rep'), may hold values from -200 to 200, as said below
- tile_corner: float32 [2, 4, 256, 2], P(None, 'rep', 'row'), may hold values from 0 to 240
- tile_owner: int32 [2, 4, 256, 4], P(None, 'rep', 'row'), may hold values from 0 to 63, all different within a row; in each aligned block of 4 rows (0 to 3, 4 to 7, ..., all dimensions but the last counted through in order) at most 2 rows name the same one
- tile_block: int32 [2, 4, 256, 4], P(None, 'rep', 'row'), may hold values from 0 to 31
- depth_order: int32 [2, 4, 256, 512], P(None, 'rep', 'row'), may hold values from 0 to 511, each once within a row
- targets: float32 [2, 4, 256, 3, 256], P(None, 'rep', 'row'), may hold values from 0 to 1
- migration: int32 [64, 2, 2], P('row'), may hold values from 0 to 31, as said below
Outputs:
- new_params: float32 [59, 262144], P(None, 'row')
- new_first: float32 [59, 262144], P(None, 'row')
- new_second: float32 [59, 262144], P(None, 'row')
- rendered: float32 [2, 4, 256, 3, 256], P(None, 'rep', 'row')
Inputs may be any that keep to these rules, and one draw needn't show every extreme that they name: `tile_owner`: each tile names 4 different owners; among the tiles of one device no owner is named more than 2 times. `depth_order`: each tile's row is a permutation. `migration`: the (4) entries of one owner are different blocks. `params`: row 6 lies in [1, 2]; rows 3 to 5 in [-1.9, -0.7]; row 10 in [2, 4]. `camera`: entries 8 to 10 form a unit vector.
All inputs are finite; a program needn't handle non-finite values.
Results may differ from a plain program's by a relative error of at most 0.0003.
Values sent between devices are 32-bit elements; how exact they have to be, the bound alone decides.
A program may use at most 64 MiB of HBM per device.

v0:
```python
import math

import jax
import jax.numpy as jnp
from jax import lax
from jax.sharding import PartitionSpec as P

P_SIZE = 59
BLOCK = 128
LISTB = 4
PIX = 256
ITERS = 2
MIGH = 2
DEPTH = 512


harm_zero = 0.28209479177387814
harm_one = 0.4886025119029199
harm_two = (
    1.0925484305920792,
    -1.0925484305920792,
    0.31539156525252005,
    -1.0925484305920792,
    0.5462742152960396,
)
harm_three = (
    -0.5900435899266435,
    2.890611442640554,
    -0.4570457994644658,
    0.3731763325901154,
    -0.4570457994644658,
    1.445305721320277,
    -0.5900435899266435,
)
learn_rate = 0.01
adam_epsilon = 1e-08


def extended(block, sides, width):
    for axis, dim in sides:
        count = lax.axis_size(axis)
        forward = [(i, i + 1) for i in range(count - 1)]
        forward.append((count - 1, 0))
        backward = [(target, source) for source, target in forward]
        low = lax.ppermute(
            lax.slice_in_dim(block, block.shape[dim] - width, None, axis=dim), axis, forward
        )
        high = lax.ppermute(lax.slice_in_dim(block, 0, width, axis=dim), axis, backward)
        block = jnp.concatenate([low, block, high], axis=dim)
    return block


def harmonics(facing):
    face_x, face_y, face_z = (facing[0], facing[1], facing[2])
    face_xx, face_yy, face_zz = (face_x * face_x, face_y * face_y, face_z * face_z)
    terms = [
        harm_zero + 0.0 * face_x,
        -harm_one * face_y,
        harm_one * face_z,
        -harm_one * face_x,
        harm_two[0] * face_x * face_y,
        harm_two[1] * face_y * face_z,
        harm_two[2] * (2.0 * face_zz - face_xx - face_yy),
        harm_two[3] * face_x * face_z,
        harm_two[4] * (face_xx - face_yy),
        harm_three[0] * face_y * (3.0 * face_xx - face_yy),
        harm_three[1] * face_x * face_y * face_z,
        harm_three[2] * face_y * (4.0 * face_zz - face_xx - face_yy),
        harm_three[3] * face_z * (2.0 * face_zz - 3.0 * face_xx - 3.0 * face_yy),
        harm_three[4] * face_x * (4.0 * face_zz - face_xx - face_yy),
        harm_three[5] * face_z * (face_xx - face_yy),
        harm_three[6] * face_x * (face_xx - 3.0 * face_yy),
    ]
    return jnp.stack(terms)


def project(params, camera_now):
    means = params[0:3]
    scales = jnp.exp(params[3:6])
    quats = params[6:10]
    quats = quats / jnp.sqrt(jnp.sum(quats * quats, axis=0, keepdims=True))
    quat_w, quat_x, quat_y, quat_z = (quats[0], quats[1], quats[2], quats[3])
    rotation = [
        [
            1.0 - 2.0 * (quat_y * quat_y + quat_z * quat_z),
            2.0 * (quat_x * quat_y - quat_w * quat_z),
            2.0 * (quat_x * quat_z + quat_w * quat_y),
        ],
        [
            2.0 * (quat_x * quat_y + quat_w * quat_z),
            1.0 - 2.0 * (quat_x * quat_x + quat_z * quat_z),
            2.0 * (quat_y * quat_z - quat_w * quat_x),
        ],
        [
            2.0 * (quat_x * quat_z - quat_w * quat_y),
            2.0 * (quat_y * quat_z + quat_w * quat_x),
            1.0 - 2.0 * (quat_x * quat_x + quat_y * quat_y),
        ],
    ]
    affine = [
        [camera_now[0], camera_now[1], camera_now[2]],
        [camera_now[3], camera_now[4], camera_now[5]],
    ]
    spread = [
        [
            (
                affine[i][0] * rotation[0][k]
                + affine[i][1] * rotation[1][k]
                + affine[i][2] * rotation[2][k]
            )
            * scales[k]
            for k in range(3)
        ]
        for i in range(2)
    ]
    cov_xx = (
        spread[0][0] * spread[0][0]
        + spread[0][1] * spread[0][1]
        + spread[0][2] * spread[0][2]
        + 0.3
    )
    cov_yy = (
        spread[1][0] * spread[1][0]
        + spread[1][1] * spread[1][1]
        + spread[1][2] * spread[1][2]
        + 0.3
    )
    cov_xy = spread[0][0] * spread[1][0] + spread[0][1] * spread[1][1] + spread[0][2] * spread[1][2]
    determinant = cov_xx * cov_yy - cov_xy * cov_xy
    centre_x = (
        affine[0][0] * means[0] + affine[0][1] * means[1] + affine[0][2] * means[2] + camera_now[6]
    )
    centre_y = (
        affine[1][0] * means[0] + affine[1][1] * means[1] + affine[1][2] * means[2] + camera_now[7]
    )
    basis = harmonics(camera_now[8:11])
    colours = 0.5 + jnp.einsum(
        "k,kcg->cg", basis, params[11:59].reshape(16, 3, -1), precision=lax.Precision.HIGHEST
    )
    opacity = jax.nn.sigmoid(params[10])
    geometry = jnp.stack(
        [centre_x, centre_y, cov_yy / determinant, -cov_xy / determinant, cov_xx / determinant]
    )
    return jnp.concatenate([geometry, colours, opacity[None]], axis=0)


def render(splat_rows, corner, strict_upper):
    side = math.isqrt(PIX)
    pixels = jnp.arange(PIX, dtype=jnp.int32)
    pos_x = corner[0] + (pixels % side).astype(jnp.float32) + 0.5
    pos_y = corner[1] + (pixels // side).astype(jnp.float32) + 0.5
    gap_x = pos_x[:, None] - splat_rows[0][None, :]
    gap_y = pos_y[:, None] - splat_rows[1][None, :]
    exponent = 0.5 * (
        splat_rows[2] * gap_x * gap_x
        + 2.0 * splat_rows[3] * gap_x * gap_y
        + splat_rows[4] * gap_y * gap_y
    )
    alphas = splat_rows[8] * jnp.exp(-exponent)
    log_keep = jnp.log1p(-alphas).reshape(PIX, DEPTH // BLOCK, BLOCK)
    inside = jnp.einsum("pbi,ij->pbj", log_keep, strict_upper, precision=lax.Precision.HIGHEST)
    totals = jnp.sum(log_keep, axis=2)
    before = jnp.cumsum(totals, axis=1) - totals
    transmit = jnp.exp(inside + before[:, :, None]).reshape(PIX, DEPTH)
    return jnp.einsum(
        "cn,pn->cp", splat_rows[5:8], alphas * transmit, precision=lax.Precision.HIGHEST
    )


def slot_plan(owner_list, block_list, owners, capacity):
    flat_owner = owner_list.reshape(-1)
    hits = (flat_owner[:, None] == jnp.arange(owners, dtype=jnp.int32)[None, :]).astype(jnp.int32)
    earlier = jnp.cumsum(hits, axis=0) - hits
    rank_in = jnp.sum(earlier * hits, axis=1)
    slot_place = flat_owner * capacity + rank_in
    wanted_list = (
        jnp.full((owners * capacity,), -1, jnp.int32).at[slot_place].set(block_list.reshape(-1))
    )
    return (slot_place, wanted_list)


def serve(projected, asked_blocks, blk_dev):
    grid = projected.reshape(9, blk_dev, BLOCK)
    chosen = jnp.take(grid, jnp.maximum(asked_blocks, 0), axis=1)
    return jnp.where((asked_blocks >= 0)[None, :, None], chosen, 0.0)


def adam_step(values, moment_one, moment_two, gradient):
    moment_one = 0.9 * moment_one + 0.1 * gradient
    moment_two = 0.999 * moment_two + 0.001 * gradient * gradient
    values = values - learn_rate * moment_one / (jnp.sqrt(moment_two) + adam_epsilon)
    return (values, moment_one, moment_two)


def local(
    params,
    first_moment,
    second_moment,
    camera,
    tile_corner,
    tile_owner,
    tile_block,
    depth_order,
    targets,
    migration,
):
    owners = lax.axis_size("row")
    local_gauss = params.shape[1]
    blk_dev = local_gauss // BLOCK
    tiles_dev = tile_owner.shape[2]
    requests = tiles_dev * LISTB
    capacity = max(2, 2 * ((requests + owners - 1) // owners))
    strict_upper = (jnp.arange(BLOCK)[:, None] < jnp.arange(BLOCK)[None, :]).astype(jnp.float32)
    current = params
    moment_one = first_moment
    moment_two = second_moment
    plans = [
        slot_plan(tile_owner[step_index, 0], tile_block[step_index, 0], owners, capacity)
        for step_index in range(ITERS)
    ]

    def one_tile(splat_rows, corner, target):
        picture, tile_back = jax.vjp(lambda r: render(r, corner, strict_upper), splat_rows)
        return (picture, tile_back(picture - target)[0])

    def paired(array):
        return array.reshape((tiles_dev // 2, 2) + array.shape[1:])

    pictures = []
    for step_index in range(ITERS):
        camera_now = camera[step_index, 0]
        projected, pullback = jax.vjp(lambda p: project(p, camera_now), current)
        slot_place = plans[step_index][0]
        asked_blocks = lax.all_to_all(
            plans[step_index][1], "row", split_axis=0, concat_axis=0, tiled=True
        )
        arrived = lax.all_to_all(
            serve(projected, asked_blocks, blk_dev), "row", split_axis=1, concat_axis=1, tiled=True
        )
        listed = jnp.take(arrived, slot_place, axis=1)
        tile_rows = jnp.transpose(listed.reshape(9, tiles_dev, DEPTH), (1, 0, 2))
        orders = depth_order[step_index, 0]
        sorted_rows = jnp.take_along_axis(tile_rows, orders[:, None, :], axis=2)
        picture, sorted_grads = lax.map(
            lambda pieces: jax.vmap(one_tile)(pieces[0], pieces[1], pieces[2]),
            (
                paired(sorted_rows),
                paired(tile_corner[step_index, 0]),
                paired(targets[step_index, 0]),
            ),
        )
        pictures.append(picture.reshape(tiles_dev, 3, PIX))
        sorted_grads = sorted_grads.reshape(tiles_dev, 9, DEPTH)
        list_grads = jax.vmap(lambda g, o: jnp.zeros_like(g).at[:, o].set(g))(sorted_grads, orders)
        request_grads = jnp.transpose(list_grads, (1, 0, 2)).reshape(9, requests * BLOCK)
        outgoing = (
            jnp.zeros((9, owners * capacity, BLOCK), jnp.float32)
            .at[:, slot_place]
            .set(request_grads.reshape(9, requests, BLOCK))
        )
        returned_grads = lax.all_to_all(outgoing, "row", split_axis=1, concat_axis=1, tiled=True)
        pick_table = (
            asked_blocks[:, None] == jnp.arange(blk_dev, dtype=jnp.int32)[None, :]
        ).astype(jnp.float32)
        row_grads = jnp.einsum(
            "csb,sk->ckb", returned_grads, pick_table, precision=lax.Precision.HIGHEST
        ).reshape(9, local_gauss)
        gradient = pullback(row_grads)[0]
        summed_grad = lax.psum(gradient, "rep")
        current, moment_one, moment_two = adam_step(current, moment_one, moment_two, summed_grad)
    stacked = jnp.stack([current, moment_one, moment_two]).reshape(3, P_SIZE, blk_dev, BLOCK)
    own_list = migration[0]
    leaving = jnp.take(stacked, own_list.reshape(-1), axis=2)
    neighbours = extended(leaving, (("row", 2),), MIGH)
    from_left = neighbours[:, :, 0:MIGH]
    from_right = neighbours[:, :, 3 * MIGH : 4 * MIGH]
    stacked = stacked.at[:, :, own_list[0]].set(from_left)
    stacked = stacked.at[:, :, own_list[1]].set(from_right)
    stacked = stacked.reshape(3, P_SIZE, local_gauss)
    return (stacked[0], stacked[1], stacked[2], jnp.stack(pictures)[:, None])


def solution(mesh):
    return jax.shard_map(
        local,
        mesh=mesh,
        in_specs=(
            P(None, "row"),
            P(None, "row"),
            P(None, "row"),
            P(None, "rep", None),
            P(None, "rep", "row", None),
            P(None, "rep", "row", None),
            P(None, "rep", "row", None),
            P(None, "rep", "row", None),
            P(None, "rep", "row", None, None),
            P("row", None, None),
        ),
        out_specs=(
            P(None, "row"),
            P(None, "row"),
            P(None, "row"),
            P(None, "rep", "row", None, None),
        ),
        check_vma=False,
    )
```

profile of v0, /device:TPU:2, one launch (start us, length us, event | category | flops | bytes accessed | tf_op | source)
XLA Modules:
  0.0 539.3 jit_solution(14723168167931766713)
XLA Ops:
  11.7 12.1 %all-to-all-start = ((s32[64,2,1]{1,2,0:T(1,128)}), s32[64,2,1]{1,2,0:T(1,128)S(1)}, u32[]{:S(2)}, u32[]{:S(2)}) async-start(s32[64,2,1]{1,2,0:T(1,128)} %bitcast.2), calls=%async_computation | async-start | bytes 65536 | tf_op jit(solution)/shard_map/all_to_all | solution.py:234
  54.6 6.3 %add_divide_fusion = (f32[1,4096]{1,0:T(1,128)S(1)}, f32[1,32,128]{2,0,1:T(1,128)S(1)}, f32[1,32,128]{2,0,1:T(1,128)S(1)}) fusion(f32[59,4096]{1,0:T(8,128)} %param.20, f32[]{:T(128)} %bitcast.10, f32[]{:T(128)} %bitcast.9, f32[]{:T(128)} %bitcast.8, f32[]{:T(128)} %bitcast.7, f32[]{:T(128)} %bitcast.15, f32[]{:T(128)} %bitcast.14, f32[]{:T(128)} %bitcast.13, ...), kind=kLoop, calls=%fused_computation.378 | loop fusion | flops 61440 | bytes 114720 | tf_op jit(solution)/shard_map/jvp()/div | solution.py:140
  61.0 5.0 divide_bitcast_fusion.3
  72.1 10.3 %all-to-all-start.1 = ((f32[9,128,128]{2,0,1:T(8,128)}), f32[9,128,128]{2,0,1:T(8,128)S(1)}, u32[]{:S(2)}, u32[]{:S(2)}) async-start(f32[9,128,128]{2,0,1:T(8,128)} %bitcast_select_fusion.1), calls=%async_computation.1 | async-start | bytes 2097152 | tf_op jit(solution)/shard_map/all_to_all | solution.py:237
  85.0 26.3 %all-to-all-done.1 = f32[9,128,128]{2,0,1:T(8,128)S(1)} async-done(((f32[9,128,128]{2,0,1:T(8,128)}), f32[9,128,128]{2,0,1:T(8,128)S(1)}, u32[]{:S(2)}, u32[]{:S(2)}) %all-to-all-start.1) | async-done | bytes 589856 | tf_op jit(solution)/shard_map/all_to_all | solution.py:237
  112.3 13.0 %gather_fusion.3 = f32[2048,9]{1,0:T(8,128)S(1)} fusion(f32[4,9,512]{1,2,0:T(8,128)S(1)} %bitcast.501, s32[2048]{0:T(1024)S(1)} %bitcast.497), kind=kCustom, calls=%fused_computation.2.clone | custom fusion | bytes 163840 | tf_op jit(solution)/shard_map/jit(take_along_axis)/gather | solution.py:243
  127.3 37.4 %while.32 = (s32[]{:T(128)}, f32[2,2,3,256]{3,2,1,0:T(4,128)}, f32[2,2,9,512]{3,2,1,0:T(8,128)}, f32[2,2,9,512]{3,2,1,0:T(8,128)S(1)}, f32[2,2,2]{2,1,0:T(2,128)...) while((s32[]{:T(128)}, f32[2,2,3,256]{3,2,1,0:T(4,128)}, ...), condition=%wide.region_15.19_spmd.clone.clone, body=%wide.region_4.18_spmd.clone.clone.sunk | while | flops 868624896 | bytes 29688096 | solution.py:244
  166.0 6.4 %scatter_custom_fusion.6 = f32[9,2048]{0,1:T(8,128)S(1)} fusion(s32[2048]{0:T(1024)} %bitcast.591, f32[2048,9]{1,0:T(8,128)S(1)} %bitcast.523, f32[]{:T(128)} %constant.295.clone.1), kind=kCustom, calls=%fused_computation.240 | custom fusion | bytes 74240
  176.2 5.6 %all-to-all-start.2 = ((f32[9,128,128]{2,0,1:T(8,128)}), f32[9,128,128]{2,0,1:T(8,128)S(1)}, u32[]{:S(2)}, u32[]{:S(2)}) async-start(f32[9,128,128]{2,0,1:T(8,128)} %scatter_fusion), calls=%async_computation.2 | async-start | bytes 2097152 | tf_op jit(solution)/shard_map/all_to_all | solution.py:261
  184.1 26.5 %all-to-all-done.2 = f32[9,128,128]{2,0,1:T(8,128)S(1)} async-done(((f32[9,128,128]{2,0,1:T(8,128)}), f32[9,128,128]{2,0,1:T(8,128)S(1)}, u32[]{:S(2)}, u32[]{:S(2)}) %all-to-all-start.2) | async-done | bytes 589856 | tf_op jit(solution)/shard_map/all_to_all | solution.py:261
  211.1 4.5 fusion.160
  233.1 5.6 %all-to-all-start.3 = ((s32[64,2,1]{1,2,0:T(1,128)}), s32[64,2,1]{1,2,0:T(1,128)S(1)}, u32[]{:S(2)}, u32[]{:S(2)}) async-start(s32[64,2,1]{1,2,0:T(1,128)} %bitcast.78), calls=%async_computation.3 | async-start | bytes 65536 | tf_op jit(solution)/shard_map/all_to_all | solution.py:234
  259.5 18.7 %all-reduce.59.cloned.1.call-done = f32[59,4096]{1,0:T(8,128)} async-done(((f32[59,4096]{1,0:T(8,128)}), f32[59,4096]{1,0:T(8,128)}) %all-reduce.59.cloned.1.call-update) | async-done | bytes 966672 | tf_op jit(solution)/shard_map/psum | solution.py:269
  282.9 4.9 fusion.124
  287.9 4.7 divide_bitcast_fusion
  294.9 10.5 %all-to-all-start.4 = ((f32[9,128,128]{2,0,1:T(8,128)}), f32[9,128,128]{2,0,1:T(8,128)S(1)}, u32[]{:S(2)}, u32[]{:S(2)}) async-start(f32[9,128,128]{2,0,1:T(8,128)} %bitcast_select_fusion), calls=%async_computation.4 | async-start | bytes 2097152 | tf_op jit(solution)/shard_map/all_to_all | solution.py:237
  306.8 27.5 %all-to-all-done.4 = f32[9,128,128]{2,0,1:T(8,128)S(1)} async-done(((f32[9,128,128]{2,0,1:T(8,128)}), f32[9,128,128]{2,0,1:T(8,128)S(1)}, u32[]{:S(2)}, u32[]{:S(2)}) %all-to-all-start.4) | async-done | bytes 589856 | tf_op jit(solution)/shard_map/all_to_all | solution.py:237
  335.3 13.0 %gather_fusion.6 = f32[2048,9]{1,0:T(8,128)S(1)} fusion(f32[4,9,512]{1,2,0:T(8,128)S(1)} %bitcast.503, s32[2048]{0:T(1024)S(1)} %bitcast.498), kind=kCustom, calls=%fused_computation.5.clone | custom fusion | bytes 163840 | tf_op jit(solution)/shard_map/jit(take_along_axis)/gather | solution.py:243
  350.3 36.0 %while.33 = (s32[]{:T(128)}, f32[2,2,3,256]{3,2,1,0:T(4,128)}, f32[2,2,9,512]{3,2,1,0:T(8,128)}, f32[2,2,9,512]{3,2,1,0:T(8,128)S(1)}, f32[2,2,2]{2,1,0:T(2,128)...) while((s32[]{:T(128)}, f32[2,2,3,256]{3,2,1,0:T(4,128)}, ...), condition=%wide.region_35.39_spmd.clone.clone, body=%wide.region_24.38_spmd.clone.clone.sunk | while | flops 868624896 | bytes 29788504 | solution.py:244
  387.6 6.2 %scatter_custom_fusion.7 = f32[9,2048]{0,1:T(8,128)S(1)} fusion(s32[2048]{0:T(1024)} %bitcast.592, f32[2048,9]{1,0:T(8,128)S(1)} %bitcast.524, f32[]{:T(128)} %constant.295.clone.1), kind=kCustom, calls=%fused_computation.238 | custom fusion | bytes 74240
  395.2 34.3 %all_to_all.38 = f32[9,128,128]{2,0,1:T(8,128)S(1)} all-to-all(f32[9,128,128]{2,0,1:T(8,128)S(1)} %scatter_fusion.1), channel_id=1, replica_groups=mesh['row'=64,'rep'=4] {'row'}, dimensions={1} | all-to-all | bytes 1179648 | tf_op jit(solution)/shard_map/all_to_all | solution.py:261
  435.7 4.8 add_add_fusion.8
  456.8 46.9 %all-reduce.61.cloned.1.call-done = f32[59,4096]{1,0:T(8,128)} async-done(((f32[59,4096]{1,0:T(8,128)}), f32[59,4096]{1,0:T(8,128)}) %all-reduce.61.cloned.1.call-update) | async-done | bytes 966672 | tf_op jit(solution)/shard_map/psum | solution.py:269
  515.6 6.3 %collective-permute-done = f32[3,59,2,128]{3,1,0,2:T(8,128)S(1)} collective-permute-done((f32[3,59,2,128]{3,1,0,2:T(8,128)S(1)}, f32[3,59,2,128]{3,1,0,2:T(8,128)S(1)}, u32[]{:S(2)}, u32[]{:S(2)}) %collective-permute-start) | collective-permute-done | bytes 181280 | tf_op jit(solution)/shard_map/ppermute | solution.py:45
  (536 shorter events, 183.3 us)
Async XLA Ops:
  7.2 58.8 %copy-start.79 = (f32[2,1,4,2]{2,3,1,0:T(2,128)S(1)}, f32[2,1,4,2]{2,3,1,0:T(2,128)}, u32[]{:S(2)}) copy-start(f32[2,1,4,2]{2,3,1,0:T(2,128)} %param.24) | copy-start | bytes 196
  10.3 57.7 %copy-start.84 = (s32[16]{0:T(128)}, s32[16]{0:T(128)S(1)}, u32[]{:S(2)}) copy-start(s32[16]{0:T(128)S(1)} %fusion.143) | copy-start | bytes 196
  11.7 56.3 %all-to-all-start = ((s32[64,2,1]{1,2,0:T(1,128)}), s32[64,2,1]{1,2,0:T(1,128)S(1)}, u32[]{:S(2)}, u32[]{:S(2)}) async-start(s32[64,2,1]{1,2,0:T(1,128)} %bitcast.2), calls=%async_computation | async-start | bytes 65536 | tf_op jit(solution)/shard_map/all_to_all | solution.py:234
  72.1 39.2 %all-to-all-start.1 = ((f32[9,128,128]{2,0,1:T(8,128)}), f32[9,128,128]{2,0,1:T(8,128)S(1)}, u32[]{:S(2)}, u32[]{:S(2)}) async-start(f32[9,128,128]{2,0,1:T(8,128)} %bitcast_select_fusion.1), calls=%async_computation.1 | async-start | bytes 2097152 | tf_op jit(solution)/shard_map/all_to_all | solution.py:237
  172.9 54.1 %copy-start.48 = (f32[1,4096]{1,0:T(1,128)S(1)}, f32[1,4096]{1,0:T(1,128)}, u32[]{:S(2)}) copy-start(f32[1,4096]{1,0:T(1,128)} %get-tuple-element.429) | copy-start | bytes 49156
  172.9 54.2 %copy-start.47 = (f32[1,4096]{1,0:T(1,128)S(1)}, f32[1,4096]{1,0:T(1,128)}, u32[]{:S(2)}) copy-start(f32[1,4096]{1,0:T(1,128)} %get-tuple-element.422) | copy-start | bytes 49156
  172.9 54.2 %copy-start.46 = (f32[1,4096]{1,0:T(1,128)S(1)}, f32[1,4096]{1,0:T(1,128)}, u32[]{:S(2)}) copy-start(f32[1,4096]{1,0:T(1,128)} %get-tuple-element.424) | copy-start | bytes 49156
  172.9 54.2 %copy-start.4 = (f32[59,4096]{1,0:T(8,128)S(1)}, f32[59,4096]{1,0:T(8,128)}, u32[]{:S(2)}) copy-start(f32[59,4096]{1,0:T(8,128)} %param.20) | copy-start | bytes 2899972
  172.9 54.2 %copy-start.32 = (f32[4096]{0:T(1024)S(1)}, f32[4096]{0:T(1024)}, u32[]{:S(2)}) copy-start(f32[4096]{0:T(1024)} %get-tuple-element.523) | copy-start | bytes 49156
  172.9 54.3 %copy-start.21 = (f32[4096]{0:T(1024)S(1)}, f32[4096]{0:T(1024)}, u32[]{:S(2)}) copy-start(f32[4096]{0:T(1024)} %copy-done.20) | copy-start | bytes 49156
  172.9 54.4 %copy-start.18 = (f32[4096]{0:T(1024)S(1)}, f32[4096]{0:T(1024)}, u32[]{:S(2)}) copy-start(f32[4096]{0:T(1024)} %copy-done.17) | copy-start | bytes 49156
  174.0 53.4 %copy-start.71 = (f32[16]{0:T(128)S(1)}, f32[16]{0:T(128)}, u32[]{:S(2)}) copy-start(f32[16]{0:T(128)} %copy-done.70) | copy-start | bytes 196
  176.2 34.4 %all-to-all-start.2 = ((f32[9,128,128]{2,0,1:T(8,128)}), f32[9,128,128]{2,0,1:T(8,128)S(1)}, u32[]{:S(2)}, u32[]{:S(2)}) async-start(f32[9,128,128]{2,0,1:T(8,128)} %scatter_fusion), calls=%async_computation.2 | async-start | bytes 2097152 | tf_op jit(solution)/shard_map/all_to_all | solution.py:261
  181.8 96.4 %all-reduce.59.cloned.1.call-start = ((), (), s32[]{:S(2)}) async-start(), calls=%async_computation.6 | async-start | bytes 2097152 | tf_op jit(solution)/shard_map/psum | solution.py:269
  233.1 24.9 %all-to-all-start.3 = ((s32[64,2,1]{1,2,0:T(1,128)}), s32[64,2,1]{1,2,0:T(1,128)S(1)}, u32[]{:S(2)}, u32[]{:S(2)}) async-start(s32[64,2,1]{1,2,0:T(1,128)} %bitcast.78), calls=%async_computation.3 | async-start | bytes 65536 | tf_op jit(solution)/shard_map/all_to_all | solution.py:234
  294.9 53.5 %copy-start.64 = (pred[4,512]{1,0:T(4,128)(4,1)S(1)}, pred[4,512]{1,0:T(4,128)(4,1)}, u32[]{:S(2)}) copy-start(pred[4,512]{1,0:T(4,128)(4,1)} %get-tuple-element.515) | copy-start | bytes 6148
  294.9 39.4 %all-to-all-start.4 = ((f32[9,128,128]{2,0,1:T(8,128)}), f32[9,128,128]{2,0,1:T(8,128)S(1)}, u32[]{:S(2)}, u32[]{:S(2)}) async-start(f32[9,128,128]{2,0,1:T(8,128)} %bitcast_select_fusion), calls=%async_computation.4 | async-start | bytes 2097152 | tf_op jit(solution)/shard_map/all_to_all | solution.py:237
  305.4 198.3 %all-reduce.61.cloned.1.call-start = ((), (), s32[]{:S(2)}) async-start(), calls=%async_computation.7 | async-start | bytes 2097152 | tf_op jit(solution)/shard_map/psum | solution.py:269
  394.1 56.7 %copy-start.3 = (f32[59,4096]{1,0:T(8,128)S(1)}, f32[59,4096]{1,0:T(8,128)}, u32[]{:S(2)}) copy-start(f32[59,4096]{1,0:T(8,128)} %copy-done.2) | copy-start | bytes 2899972
  394.1 57.6 %copy-start.23 = (f32[4096]{0:T(1024)S(1)}, f32[4096]{0:T(1024)}, u32[]{:S(2)}) copy-start(f32[4096]{0:T(1024)} %copy-done.22) | copy-start | bytes 49156
  395.2 57.3 %copy-start.73 = (f32[16]{0:T(128)S(1)}, f32[16]{0:T(128)}, u32[]{:S(2)}) copy-start(f32[16]{0:T(128)} %copy-done.72) | copy-start | bytes 196
  452.5 51.2 %copy-start.6 = (f32[59,4096]{1,0:T(8,128)S(1)}, f32[59,4096]{1,0:T(8,128)}, u32[]{:S(2)}) copy-start(f32[59,4096]{1,0:T(8,128)} %param.21) | copy-start | bytes 2899972
  509.5 14.9 %collective-permute-start.1 = (f32[3,59,2,128]{3,1,0,2:T(8,128)S(1)}, f32[3,59,2,128]{3,1,0,2:T(8,128)S(1)}, u32[]{:S(2)}, u32[]{:S(2)}) collective-permute-start(f32[3,59,2,128]{3,1,0,2:T(8,128)S(1)} %get-tuple-element.479), channel_id=1, source_target_pairs={{4,0},{8,4},{12,8},{16,12},{20,16},{24,20},{28,24},{32,28},{36,32}... | collective-permute-start | bytes 543752 | tf_op jit(solution)/shard_map/ppermute | solution.py:48
  513.5 8.4 %collective-permute-start = (f32[3,59,2,128]{3,1,0,2:T(8,128)S(1)}, f32[3,59,2,128]{3,1,0,2:T(8,128)S(1)}, u32[]{:S(2)}, u32[]{:S(2)}) collective-permute-start(f32[3,59,2,128]{3,1,0,2:T(8,128)S(1)} %get-tuple-element.480), channel_id=1, source_target_pairs={{0,4},{4,8},{8,12},{12,16},{16,20},{20,24},{24,28},{28,32},{32,36}... | collective-permute-start | bytes 543752 | tf_op jit(solution)/shard_map/ppermute | solution.py:45
  (84 other events, 1437.7 us)
Sparse Core Ops, SparseCore 0:
  231.7 46.4 all-reduce.58
  456.8 46.8 all-reduce.60
where the time goes:
time: 549 us; the launch traced here: 539 us
  waiting for transfers between devices  152 us (28%)
  other arithmetic  106 us (19%)
  local copies, waits for them, and re-layouts  99.7 us (18%)
  between operations  55.4 us (10%)
  starting transfers between devices  48 us (9%)
  matrix products  42.3 us (8%)
  blocking collectives  34.3 us (6%)
    psum x2, waiting for transfers between devices, local(): summed_grad = lax.psum(gradient, 'rep')  65.6 us
    all_to_all x2, waiting for transfers between devices, local(): lax.all_to_all(serve(projected, asked_blocks, blk_dev), 'row', split_axis...  53.7 us
    all_to_all x1, blocking collectives, local(): lax.all_to_all(outgoing, 'row', split_axis=1, concat_axis=1, tiled=True)  34.3 us
    dot_general x12, matrix products, render(): jnp.einsum('cn,pn->cp', splat_rows[5:8], alphas * transmit, precision=lax...  27 us
    all_to_all x1, waiting for transfers between devices, local(): lax.all_to_all(outgoing, 'row', split_axis=1, concat_axis=1, tiled=True)  26.5 us
    gather x2, local copies, waits for them, and re-layouts, local(): sorted_rows = jnp.take_along_axis(tile_rows, orders[:, None, :], axis=2)  26.1 us
    unnamed x190, local copies, waits for them, and re-layouts  23.6 us
    all_to_all x2, starting transfers between devices, local(): lax.all_to_all(serve(projected, asked_blocks, blk_dev), 'row', split_axis...  20.8 us
  transfers between devices with their start and end apart: 9, of which 6 were waited for; matrix products, arithmetic and copies ran while one was open for 7% of the time, Pallas kernels for 0%

commit v1 on v0

v1 whole, which is shorter than its diff:
```python
import functools

import jax
import jax.numpy as jnp
from jax import lax
from jax.experimental import pallas as pl
from jax.experimental.pallas import tpu as pltpu
from jax.sharding import PartitionSpec as P

P_SIZE = 59
BLOCK = 128
LISTB = 4
PIX = 256
SIDE = 16
ITERS = 2
MIGH = 2
DEPTH = 512
NINE = 9
CAP = 2
STRIDE = 64
PAIR = 24
SENT = 18
MESH = pl.DeviceIdType.MESH
f32 = jnp.float32
bf16 = jnp.bfloat16

harm_zero = 0.28209479177387814
harm_one = 0.4886025119029199
harm_two = (
    1.0925484305920792,
    -1.0925484305920792,
    0.31539156525252005,
    -1.0925484305920792,
    0.5462742152960396,
)
harm_three = (
    -0.5900435899266435,
    2.890611442640554,
    -0.4570457994644658,
    0.3731763325901154,
    -0.4570457994644658,
    1.445305721320277,
    -0.5900435899266435,
)
learn_rate = 0.01
adam_epsilon = 1e-08


def harmonics(face_x, face_y, face_z):
    face_xx, face_yy, face_zz = (face_x * face_x, face_y * face_y, face_z * face_z)
    return [
        harm_zero + 0.0 * face_x,
        -harm_one * face_y,
        harm_one * face_z,
        -harm_one * face_x,
        harm_two[0] * face_x * face_y,
        harm_two[1] * face_y * face_z,
        harm_two[2] * (2.0 * face_zz - face_xx - face_yy),
        harm_two[3] * face_x * face_z,
        harm_two[4] * (face_xx - face_yy),
        harm_three[0] * face_y * (3.0 * face_xx - face_yy),
        harm_three[1] * face_x * face_y * face_z,
        harm_three[2] * face_y * (4.0 * face_zz - face_xx - face_yy),
        harm_three[3] * face_z * (2.0 * face_zz - 3.0 * face_xx - 3.0 * face_yy),
        harm_three[4] * face_x * (4.0 * face_zz - face_xx - face_yy),
        harm_three[5] * face_z * (face_xx - face_yy),
        harm_three[6] * face_x * (face_xx - 3.0 * face_yy),
    ]


def split2(x):
    high = x.astype(bf16)
    return high, (x - high.astype(f32)).astype(bf16)


def split3(x):
    high = x.astype(bf16)
    rest = x - high.astype(f32)
    mid = rest.astype(bf16)
    return high, mid, (rest - mid.astype(f32)).astype(bf16)


def dot(a, b, dims=((1,), (0,))):
    return lax.dot_general(a, b, (dims, ((), ())), preferred_element_type=f32)


NT = ((1,), (1,))


def geometry(rows):
    scales = [jnp.exp(rows(3 + k)) for k in range(3)]
    q = [rows(6 + k) for k in range(4)]
    inverse = 1.0 / jnp.sqrt(q[0] * q[0] + q[1] * q[1] + q[2] * q[2] + q[3] * q[3])
    w, x, y, z = [v * inverse for v in q]
    rotation = [
        [1.0 - 2.0 * (y * y + z * z), 2.0 * (x * y - w * z), 2.0 * (x * z + w * y)],
        [2.0 * (x * y + w * z), 1.0 - 2.0 * (x * x + z * z), 2.0 * (y * z - w * x)],
        [2.0 * (x * z - w * y), 2.0 * (y * z + w * x), 1.0 - 2.0 * (x * x + y * y)],
    ]
    return scales, (w, x, y, z), inverse, rotation


def conic_of(affine, scales, rotation):
    spread = [
        [
            (affine[i][0] * rotation[0][k] + affine[i][1] * rotation[1][k] + affine[i][2] * rotation[2][k])
            * scales[k]
            for k in range(3)
        ]
        for i in range(2)
    ]
    s0, s1 = spread
    cov_xx = s0[0] * s0[0] + s0[1] * s0[1] + s0[2] * s0[2] + 0.3
    cov_yy = s1[0] * s1[0] + s1[1] * s1[1] + s1[2] * s1[2] + 0.3
    cov_xy = s0[0] * s1[0] + s0[1] * s1[1] + s0[2] * s1[2]
    over = 1.0 / (cov_xx * cov_yy - cov_xy * cov_xy)
    return spread, (cov_yy * over, -cov_xy * over, cov_xx * over)


def sigmoid(x):
    return 1.0 / (1.0 + jnp.exp(-x))


def kernel(
    nr,
    nx,
    nb,
    tiles,
    corner_ref,
    own_ref,
    migration_ref,
    request_ref,
    column_ref,
    camera_ref,
    order_ref,
    target_ref,
    p_hbm,
    m_hbm,
    v_hbm,
    p_out,
    m_out,
    v_out,
    picture_ref,
    p_s,
    m_s,
    v_s,
    ask_send,
    ask_recv,
    cam_recv,
    cam_smem,
    f_send,
    f_recv,
    g_send,
    g_recv,
    shared,
    mig_send,
    mig_recv,
    listing,
    listed_rows,
    picks,
    upper,
    lower,
    logs,
    alphas,
    passing,
    weight_high,
    weight_low,
    pulls,
    products,
    behind,
    request_grads,
    local_sem,
    out_sem,
    ask_ssem,
    ask_rsem,
    cam_ssem,
    cam_rsem,
    cam_sem,
    a2a_ssem,
    a2a_rsem,
    rep_ssem,
    rep_rsem,
    mig_ssem,
    mig_rsem,
):
    me = lax.axis_index("row")
    rep = lax.axis_index("rep")
    state = (p_s, m_s, v_s)

    def block_rows(ref, b):
        return ref.at[pl.ds(pl.multiple_of(STRIDE * b, 8), P_SIZE), :]

    def lanes_of(ref, b):
        return ref.at[:, pl.ds(pl.multiple_of(BLOCK * b, BLOCK), BLOCK)]

    def load_copy(a, b):
        return pltpu.make_async_copy(
            lanes_of((p_hbm, m_hbm, v_hbm)[a], b), block_rows(state[a], b), local_sem.at[a, b]
        )

    for a in range(3):
        lax.fori_loop(0, nb, lambda b, c: (load_copy(a, b).start(), c)[1], 0)

    barrier = pltpu.get_barrier_semaphore()

    def greet_row(k, c):
        pl.semaphore_signal(barrier, 1, device_id={"row": lax.rem(me + k, nr)}, device_id_type=MESH)
        return c

    def greet_rep(k, c):
        pl.semaphore_signal(barrier, 1, device_id={"rep": lax.rem(rep + k, nx)}, device_id_type=MESH)
        return c

    lax.fori_loop(1, nr, greet_row, 0)
    lax.fori_loop(1, nx, greet_rep, 0)

    asked_now = jnp.full((nr, BLOCK), -1, jnp.int32)
    lane = lax.broadcasted_iota(jnp.int32, (nr, BLOCK), 1)
    owner_id = lax.broadcasted_iota(jnp.int32, (nr, BLOCK), 0)
    requests = tiles * LISTB
    for i in range(ITERS):
        for s in range(CAP):
            match = (owner_id * CAP + s == request_ref[i : i + 1, :]) & (lane < requests)
            column = jnp.sum(
                jnp.where(match, request_ref[ITERS + i : ITERS + i + 1, :] + 1.0, 0.0), axis=1, keepdims=True
            )
            asked_now = jnp.where(lane == CAP * i + s, column.astype(jnp.int32) - 1, asked_now)
    ask_send[pl.ds(0, nr, stride=8), :] = asked_now
    cam_recv[pl.ds(pl.multiple_of(8 * rep, 8), 1), :] = camera_ref[...]

    pl.semaphore_wait(barrier, nr + nx - 2)

    def row_of(k):
        return lax.rem(me + k, nr), lax.rem(me + nr - k, nr)

    def ask_copy(k, at):
        to, _ = row_of(k)
        return pltpu.make_async_remote_copy(
            src_ref=ask_send.at[pl.ds(pl.multiple_of(8 * to, 8), 1), :],
            dst_ref=ask_recv.at[pl.ds(pl.multiple_of(8 * at, 8), 1), :],
            send_sem=ask_ssem.at[k],
            recv_sem=ask_rsem.at[k],
            device_id={"row": to},
            device_id_type=MESH,
        )

    def cam_copy(k, at):
        return pltpu.make_async_remote_copy(
            src_ref=cam_recv.at[pl.ds(pl.multiple_of(8 * rep, 8), 1), :],
            dst_ref=cam_recv.at[pl.ds(pl.multiple_of(8 * at, 8), 1), :],
            send_sem=cam_ssem.at[k],
            recv_sem=cam_rsem.at[k],
            device_id={"rep": lax.rem(rep + k, nx)},
            device_id_type=MESH,
        )

    lax.fori_loop(1, nr, lambda k, c: (ask_copy(k, me).start(), c)[1], 0)
    for k in range(1, nx):
        cam_copy(k, rep).start()
    own_ask = pl.ds(pl.multiple_of(8 * me, 8), 8)
    ask_recv[own_ask, :] = ask_send[own_ask, :]

    square = lax.broadcasted_iota(jnp.int32, (DEPTH, DEPTH), 0), lax.broadcasted_iota(jnp.int32, (DEPTH, DEPTH), 1)
    before = jnp.where(square[0] < square[1], 1.0, 0.0).astype(bf16)
    after = jnp.where(square[0] > square[1], 1.0, 0.0).astype(bf16)
    for part in range(3):
        upper[part * DEPTH : (part + 1) * DEPTH, :] = before
    for part in range(2):
        lower[part * DEPTH : (part + 1) * DEPTH, :] = after
    listed_rows[...] = jnp.zeros_like(listed_rows)

    for a in range(3):
        lax.fori_loop(0, nb, lambda b, c: (load_copy(a, b).wait(), c)[1], 0)

    def row(ref, r):
        return ref[pl.ds(r, nb, stride=STRIDE), :]

    def put_row(ref, r, x):
        ref[pl.ds(r, nb, stride=STRIDE), :] = x

    def project(i):
        cam = [own_ref[i, k] for k in range(11)]
        affine = [cam[0:3], cam[3:6]]
        rows = functools.partial(row, p_s)
        scales, _, _, rotation = geometry(rows)
        _, conic = conic_of(affine, scales, rotation)
        means = [rows(k) for k in range(3)]
        centre = [
            affine[j][0] * means[0] + affine[j][1] * means[1] + affine[j][2] * means[2] + cam[6 + j] for j in range(2)
        ]
        basis = harmonics(*cam[8:11])
        colours = []
        for k in range(3):
            total = basis[0] * rows(11 + k)
            for j in range(1, 16):
                total = total + basis[j] * rows(11 + 3 * j + k)
            colours.append(0.5 + total)
        return centre + list(conic) + colours + [sigmoid(rows(10))]

    def put_slots(ref, values):
        for s in range(CAP):
            for c in range(NINE):
                base = 8 * s + c if c < 8 else 16 + s
                ref[pl.ds(base, nr, stride=PAIR), :] = values[s * nr : (s + 1) * nr, c * BLOCK : (c + 1) * BLOCK]

    def get_slots(ref):
        columns = []
        for c in range(NINE):
            columns.append(
                jnp.concatenate(
                    [ref[pl.ds(8 * s + c if c < 8 else 16 + s, nr, stride=PAIR), :] for s in range(CAP)], axis=0
                )
            )
        return jnp.concatenate(columns, axis=1)

    def pair_rows(p):
        return pl.ds(pl.multiple_of(PAIR * p, 8), SENT)

    def slot_copy(send, recv, which, k, at):
        to, _ = row_of(k)
        return pltpu.make_async_remote_copy(
            src_ref=send.at[pair_rows(to), :],
            dst_ref=recv.at[pair_rows(at), :],
            send_sem=a2a_ssem.at[which, k],
            recv_sem=a2a_rsem.at[which, k],
            device_id={"row": to},
            device_id_type=MESH,
        )

    def exchange(send, recv, which):
        lax.fori_loop(1, nr, lambda k, c: (slot_copy(send, recv, which, k, me).start(), c)[1], 0)
        own = pl.ds(pl.multiple_of(PAIR * me, 8), PAIR)
        recv[own, :] = send[own, :]

        def arrived(k, c):
            copy = slot_copy(send, recv, which, k, row_of(k)[1])
            copy.wait_recv()
            copy.wait_send()
            return c

        lax.fori_loop(1, nr, arrived, 0)

    def render(i, recv):
        slot_lane = lax.broadcasted_iota(jnp.int32, (requests, CAP * nr), 1)
        slot_lane = CAP * lax.rem(slot_lane, nr) + slot_lane // nr
        take = jnp.where(column_ref[:, i : i + 1] == slot_lane.astype(f32), 1.0, 0.0).astype(bf16)
        pieces = split3(get_slots(recv))
        listed = dot(take, pieces[0]) + dot(take, pieces[1]) + dot(take, pieces[2])
        for c in range(NINE):
            listed_rows[pl.ds(c, requests, stride=16), :] = listed[:, BLOCK * c : BLOCK * (c + 1)]

        def one_tile(t, carry):
            for j in range(LISTB):
                listing[:, BLOCK * j : BLOCK * (j + 1)] = listed_rows[
                    pl.ds(pl.multiple_of(16 * (LISTB * t + j), 16), 16), :
                ]
            order = order_ref[pl.ds(i * tiles + t, 1), 0, :]
            pick = jnp.where(lax.broadcasted_iota(jnp.int32, (DEPTH, DEPTH), 0) == order, 1.0, 0.0).astype(bf16)
            picks[...] = pick
            parts = dot(jnp.concatenate(split3(listing[...]), axis=0), picks[...])
            splats = parts[0:16] + parts[16:32] + parts[32:48]
            centre_x, centre_y = splats[0:1], splats[1:2]
            conic_a, conic_b, conic_c = splats[2:3], splats[3:4], splats[4:5]
            opacity = splats[8:9]
            ticks = lax.broadcasted_iota(jnp.int32, (SIDE, DEPTH), 0).astype(f32)
            gap_x = (corner_ref[i, 2 * t] + ticks + 0.5) - centre_x
            gap_y = (corner_ref[i, 2 * t + 1] + ticks + 0.5) - centre_y
            along = -0.5 * conic_a * gap_x * gap_x
            cross = -conic_b * gap_y
            across = -0.5 * conic_c * gap_y * gap_y
            for y in range(SIDE):
                at = slice(SIDE * y, SIDE * (y + 1))
                alpha = opacity * jnp.exp(along + across[y : y + 1] + gap_x * cross[y : y + 1])
                alphas[at, :] = alpha
                for part, piece in enumerate(split3(jnp.log(1.0 - alpha))):
                    logs[at, part * DEPTH : (part + 1) * DEPTH] = piece
            passing[...] = dot(logs[...], upper[...])
            for y in range(SIDE):
                at = slice(SIDE * y, SIDE * (y + 1))
                through = jnp.exp(passing[at, :])
                passing[at, :] = through
                high, low = split2(alphas[at, :] * through)
                weight_high[at, :] = high
                weight_low[at, :] = low
            eight = lax.broadcasted_iota(jnp.int32, (8, 1), 0)
            paint = jnp.where(eight >= 5, splats[0:8], 0.0)
            paint_high = paint.astype(bf16).astype(f32)
            paint_low = paint - paint_high
            both = dot(jnp.concatenate([paint_high, paint_low], axis=0).astype(bf16), weight_high[...], NT)
            high_low = dot(jnp.concatenate([paint_high, paint_high], axis=0).astype(bf16), weight_low[...], NT)
            picture = both[0:8] + both[8:16] + high_low[0:8]
            picture_ref[i * tiles + t] = picture[5:8]
            residual = picture - jnp.concatenate([jnp.zeros((5, PIX), f32), target_ref[i * tiles + t]], axis=0)
            res_high = residual.astype(bf16).astype(f32)
            res_low = residual - res_high
            pull = dot(
                jnp.transpose(jnp.concatenate([res_high, res_high, res_low, res_low], axis=0)).astype(bf16),
                jnp.concatenate([paint_high, paint_low, paint_high, paint_low], axis=0).astype(bf16),
            )
            pulls[...] = pull
            both = dot(jnp.concatenate([res_high, res_low], axis=0).astype(bf16), weight_high[...])
            high_low = dot(jnp.concatenate([res_high, res_high], axis=0).astype(bf16), weight_low[...])
            colour_grads = both[0:8] + both[8:16] + high_low[0:8]
            for y in range(SIDE):
                at = slice(SIDE * y, SIDE * (y + 1))
                for part, piece in enumerate(split2(alphas[at, :] * passing[at, :] * pulls[at, :])):
                    products[at, part * DEPTH : (part + 1) * DEPTH] = piece
            behind[...] = dot(products[...], lower[...])
            sums = [jnp.zeros((SIDE, DEPTH), f32) for _ in range(3)]
            for y in range(SIDE):
                at = slice(SIDE * y, SIDE * (y + 1))
                alpha = alphas[at, :]
                felt = alpha * (passing[at, :] * pulls[at, :] - behind[at, :] / (1.0 - alpha))
                tall = felt * gap_y[y : y + 1]
                sums = [sums[0] + felt, sums[1] + tall, sums[2] + tall * gap_y[y : y + 1]]

            def over_x(v):
                return jnp.sum(v, axis=0, keepdims=True)

            felt_x = gap_x * sums[0]
            total, total_x, total_xx = over_x(sums[0]), over_x(felt_x), over_x(gap_x * felt_x)
            total_y, total_xy, total_yy = over_x(sums[1]), over_x(gap_x * sums[1]), over_x(sums[2])
            grads = jnp.concatenate(
                [
                    conic_a * total_x + conic_b * total_y,
                    conic_b * total_x + conic_c * total_y,
                    -0.5 * total_xx,
                    -total_xy,
                    -0.5 * total_yy,
                    colour_grads[5:8],
                    total / opacity,
                    jnp.zeros((7, DEPTH), f32),
                ],
                axis=0,
            )
            parts = dot(jnp.concatenate(split3(grads), axis=0), picks[...], NT)
            listed = parts[0:16] + parts[16:32] + parts[32:48]
            for j in range(LISTB):
                request_grads[pl.ds(pl.multiple_of(16 * (LISTB * t + j), 16), 16), :] = listed[
                    :, BLOCK * j : BLOCK * (j + 1)
                ]
            return carry

        lax.fori_loop(0, tiles, one_tile, 0)

    def step_up(r, gradient):
        one = 0.9 * row(m_s, r) + 0.1 * gradient
        two = 0.999 * row(v_s, r) + 0.001 * gradient * gradient
        put_row(m_s, r, one)
        put_row(v_s, r, two)
        put_row(p_s, r, row(p_s, r) - learn_rate * one / (jnp.sqrt(two) + adam_epsilon))

    def pull_back(i, shares):
        rows = functools.partial(row, p_s)
        scales, quats, inverse, rotation = geometry(rows)
        cams = [[cam_smem[8 * x, 11 * i + k] for k in range(11)] for x in range(nx)]
        turn = None
        for x in range(nx):
            cam = cams[x]
            affine = [cam[0:3], cam[3:6]]

            def share(c):
                at = (x * NINE + c) * nb
                return shares[at : at + nb, :]

            spread, (con_a, con_b, con_c) = conic_of(affine, scales, rotation)
            g_a, g_b, g_c = share(2), 0.5 * share(3), share(4)
            left_a, left_b = g_a * con_a + g_b * con_b, g_a * con_b + g_b * con_c
            right_a, right_b = g_b * con_a + g_c * con_b, g_b * con_b + g_c * con_c
            n_xx = -2.0 * (con_a * left_a + con_b * right_a)
            n_xy = -2.0 * (con_a * left_b + con_b * right_b)
            n_yy = -2.0 * (con_b * left_b + con_c * right_b)
            felt = [
                [n_xx * spread[0][k] + n_xy * spread[1][k] for k in range(3)],
                [n_xy * spread[0][k] + n_yy * spread[1][k] for k in range(3)],
            ]
            stretch = [felt[0][k] * spread[0][k] + felt[1][k] * spread[1][k] for k in range(3)]
            twist = [
                [(affine[0][j] * felt[0][k] + affine[1][j] * felt[1][k]) * scales[k] for k in range(3)]
                for j in range(3)
            ]
            moved = [affine[0][j] * share(0) + affine[1][j] * share(1) for j in range(3)]
            fade = share(8)
            if turn is None:
                stretches, turn, moves, fades = stretch, twist, moved, fade
            else:
                stretches = [u + v for u, v in zip(stretches, stretch)]
                turn = [[u + v for u, v in zip(a, b)] for a, b in zip(turn, twist)]
                moves = [u + v for u, v in zip(moves, moved)]
                fades = fades + fade
        w, x, y, z = quats
        d = turn
        unit = [
            2.0 * (z * (d[1][0] - d[0][1]) + y * (d[0][2] - d[2][0]) + x * (d[2][1] - d[1][2])),
            2.0
            * (
                y * (d[0][1] + d[1][0])
                + z * (d[0][2] + d[2][0])
                + w * (d[2][1] - d[1][2])
                - 2.0 * x * (d[1][1] + d[2][2])
            ),
            2.0
            * (
                x * (d[0][1] + d[1][0])
                + w * (d[0][2] - d[2][0])
                + z * (d[1][2] + d[2][1])
                - 2.0 * y * (d[0][0] + d[2][2])
            ),
            2.0
            * (
                w * (d[1][0] - d[0][1])
                + x * (d[0][2] + d[2][0])
                + y * (d[1][2] + d[2][1])
                - 2.0 * z * (d[0][0] + d[1][1])
            ),
        ]
        inner = unit[0] * w + unit[1] * x + unit[2] * y + unit[3] * z
        opacity = sigmoid(rows(10))
        for k in range(3):
            step_up(k, moves[k])
        for k in range(3):
            step_up(3 + k, stretches[k])
        for k in range(4):
            step_up(6 + k, (unit[k] - quats[k] * inner) * inverse)
        step_up(10, fades * opacity * (1.0 - opacity))
        bases = [harmonics(*cam[8:11]) for cam in cams]
        for k in range(3):
            felt = [shares[(x * NINE + 5 + k) * nb : (x * NINE + 6 + k) * nb, :] for x in range(nx)]
            for j in range(16):
                total = bases[0][j] * felt[0]
                for x in range(1, nx):
                    total = total + bases[x][j] * felt[x]
                step_up(11 + 3 * j + k, total)

    def share_copy(i, k, at):
        size = NINE * nb
        return pltpu.make_async_remote_copy(
            src_ref=shared.at[i, pl.ds(pl.multiple_of(size * rep, 8), size), :],
            dst_ref=shared.at[i, pl.ds(pl.multiple_of(size * at, 8), size), :],
            send_sem=rep_ssem.at[i, k],
            recv_sem=rep_rsem.at[i, k],
            device_id={"rep": lax.rem(rep + k, nx)},
            device_id_type=MESH,
        )

    asked_columns = asked_lines = None
    for i in range(ITERS):
        projected = jnp.concatenate(project(i), axis=1)
        if i == 0:

            def asked(k, c):
                copy = ask_copy(k, row_of(k)[1])
                copy.wait_recv()
                copy.wait_send()
                return c

            lax.fori_loop(1, nr, asked, 0)
            asked_all = ask_recv[pl.ds(0, nr, stride=8), :].astype(f32)
            asked_columns = asked_all
            asked_lines = jnp.transpose(
                asked_all
                if nr == BLOCK
                else jnp.concatenate([asked_all, jnp.zeros((BLOCK - nr, BLOCK), f32)], axis=0)
            )
        block_lane = lax.rem(lax.broadcasted_iota(jnp.int32, (nr, 3 * nb), 1), nb).astype(f32)
        serve = jnp.concatenate(
            [
                jnp.where(asked_columns[:, CAP * i + s : CAP * i + s + 1] == block_lane, 1.0, 0.0)
                for s in range(CAP)
            ],
            axis=0,
        ).astype(bf16)
        put_slots(f_send.at[i], dot(serve, jnp.concatenate(split3(projected), axis=0)))
        exchange(f_send.at[i], f_recv.at[i], 2 * i)
        render(i, f_recv.at[i])
        by_request = jnp.concatenate([request_grads[pl.ds(c, requests, stride=16), :] for c in range(NINE)], axis=1)
        slot_line = lax.broadcasted_iota(jnp.int32, (CAP * nr, 3 * requests), 0)
        slot_line = CAP * lax.rem(slot_line, nr) + slot_line // nr
        back = jnp.where(slot_line.astype(f32) == request_ref[i : i + 1, 0 : 3 * requests], 1.0, 0.0).astype(bf16)
        put_slots(g_send.at[i], dot(back, jnp.concatenate(split3(by_request), axis=0)))
        exchange(g_send.at[i], g_recv.at[i], 2 * i + 1)
        wanted = jnp.concatenate(
            [asked_lines[CAP * i + s : CAP * i + s + 1, 0:nr] for s in range(CAP)], axis=1
        )
        gather = jnp.where(
            lax.broadcasted_iota(jnp.int32, (nb, CAP * nr), 0).astype(f32) == wanted, 1.0, 0.0
        ).astype(bf16)
        pieces = split3(get_slots(g_recv.at[i]))
        summed = dot(gather, pieces[0]) + dot(gather, pieces[1]) + dot(gather, pieces[2])
        for c in range(NINE):
            shared[i, pl.ds(pl.multiple_of(NINE * nb * rep + nb * c, 8), nb), :] = summed[
                :, BLOCK * c : BLOCK * (c + 1)
            ]
        for k in range(1, nx):
            share_copy(i, k, rep).start()
        if i == 0:
            for k in range(1, nx):
                copy = cam_copy(k, lax.rem(rep + nx - k, nx))
                copy.wait_recv()
                copy.wait_send()
            table = pltpu.make_async_copy(cam_recv, cam_smem, cam_sem)
            table.start()
            table.wait()
        for k in range(1, nx):
            copy = share_copy(i, k, lax.rem(rep + nx - k, nx))
            copy.wait_recv()
            copy.wait_send()
        pull_back(i, shared.at[i])

    hand = MIGH * 3 * STRIDE

    def hand_copy(side):
        to = lax.rem(me + (nr - 1 if side == 0 else 1), nr)
        return pltpu.make_async_remote_copy(
            src_ref=mig_send.at[pl.ds(side * hand, hand), :],
            dst_ref=mig_recv.at[pl.ds((1 - side) * hand, hand), :],
            send_sem=mig_ssem.at[side],
            recv_sem=mig_rsem.at[side],
            device_id={"row": to},
            device_id_type=MESH,
        )

    for side in range(2):
        for j in range(MIGH):
            leaving = jnp.full((STRIDE, BLOCK), migration_ref[side, j], jnp.int32)
            for a in range(3):
                at = side * hand + (3 * j + a) * STRIDE
                chosen = state[a][0:STRIDE, :]
                for b in range(1, nb):
                    chosen = jnp.where(leaving == b, state[a][STRIDE * b : STRIDE * (b + 1), :], chosen)
                mig_send[at : at + STRIDE, :] = chosen
        hand_copy(side).start()
    for side in range(2):
        hand_copy(side).wait_recv()
        hand_copy(side).wait_send()

    def settle(b, carry):
        for a in range(3):
            at = pl.ds(pl.multiple_of(STRIDE * b, STRIDE), STRIDE)
            block = state[a][at, :]
            for side in range(2):
                for j in range(MIGH):
                    source = side * hand + (3 * j + a) * STRIDE
                    here = jnp.full((STRIDE, BLOCK), migration_ref[side, j], jnp.int32) == b
                    block = jnp.where(here, mig_recv[source : source + STRIDE, :], block)
            state[a][at, :] = block
            store_copy(a, b).start()
        return carry

    def store_copy(a, b):
        return pltpu.make_async_copy(
            block_rows(state[a], b), lanes_of((p_out, m_out, v_out)[a], b), out_sem.at[a, b]
        )

    lax.fori_loop(0, nb, settle, 0)
    for a in range(3):
        lax.fori_loop(0, nb, lambda b, c: (store_copy(a, b).wait(), c)[1], 0)


def local(
    params,
    first_moment,
    second_moment,
    camera,
    tile_corner,
    tile_owner,
    tile_block,
    depth_order,
    targets,
    migration,
):
    nr, nx = lax.axis_size("row"), lax.axis_size("rep")
    local_gauss = params.shape[1]
    nb = local_gauss // BLOCK
    tiles = tile_owner.shape[2]
    requests = tiles * LISTB
    owner = tile_owner.reshape(ITERS, requests)
    block = tile_block.reshape(ITERS, requests)
    position = jnp.arange(requests, dtype=jnp.int32)
    same = (owner[:, :, None] == owner[:, None, :]) & (position[None, :] < position[:, None])
    slot = owner * CAP + jnp.sum(same.astype(jnp.int32), axis=2)
    wide = jnp.concatenate([slot, slot, slot], axis=1).astype(f32)
    table = jnp.concatenate(
        [
            jnp.pad(wide, ((0, 0), (0, BLOCK - 3 * requests)), constant_values=-1.0),
            jnp.pad(block.astype(f32), ((0, 0), (0, BLOCK - requests))),
            jnp.zeros((8 - 2 * ITERS, BLOCK), f32),
        ],
        axis=0,
    )
    own = camera.reshape(ITERS, 11)
    packed = jnp.pad(own.reshape(1, ITERS * 11), ((0, 0), (0, BLOCK - ITERS * 11)))

    vmem = pl.BlockSpec(memory_space=pltpu.VMEM)
    smem = pl.BlockSpec(memory_space=pltpu.SMEM)
    hbm = pl.BlockSpec(memory_space=pl.ANY)
    size = jax.ShapeDtypeStruct((P_SIZE, local_gauss), f32)
    dma = pltpu.SemaphoreType.DMA
    new_params, new_first, new_second, pictures = pl.pallas_call(
        functools.partial(kernel, nr, nx, nb, tiles),
        out_shape=(size, size, size, jax.ShapeDtypeStruct((ITERS * tiles, 3, PIX), f32)),
        in_specs=[smem] * 3 + [vmem] * 5 + [hbm] * 3,
        out_specs=(hbm, hbm, hbm, vmem),
        scratch_shapes=[
            pltpu.VMEM((STRIDE * nb, BLOCK), f32),
            pltpu.VMEM((STRIDE * nb, BLOCK), f32),
            pltpu.VMEM((STRIDE * nb, BLOCK), f32),
            pltpu.VMEM((8 * nr, BLOCK), jnp.int32),
            pltpu.VMEM((8 * nr, BLOCK), jnp.int32),
            pltpu.VMEM((8 * nx, BLOCK), f32),
            pltpu.SMEM((8 * nx, BLOCK), f32),
            pltpu.VMEM((ITERS, PAIR * nr, BLOCK), f32),
            pltpu.VMEM((ITERS, PAIR * nr, BLOCK), f32),
            pltpu.VMEM((ITERS, PAIR * nr, BLOCK), f32),
            pltpu.VMEM((ITERS, PAIR * nr, BLOCK), f32),
            pltpu.VMEM((ITERS, nx * NINE * nb, BLOCK), f32),
            pltpu.VMEM((2 * MIGH * 3 * STRIDE, BLOCK), f32),
            pltpu.VMEM((2 * MIGH * 3 * STRIDE, BLOCK), f32),
            pltpu.VMEM((16, DEPTH), f32),
            pltpu.VMEM((16 * requests, BLOCK), f32),
            pltpu.VMEM((DEPTH, DEPTH), bf16),
            pltpu.VMEM((3 * DEPTH, DEPTH), bf16),
            pltpu.VMEM((2 * DEPTH, DEPTH), bf16),
            pltpu.VMEM((PIX, 3 * DEPTH), bf16),
            pltpu.VMEM((PIX, DEPTH), f32),
            pltpu.VMEM((PIX, DEPTH), f32),
            pltpu.VMEM((PIX, DEPTH), bf16),
            pltpu.VMEM((PIX, DEPTH), bf16),
            pltpu.VMEM((PIX, DEPTH), f32),
            pltpu.VMEM((PIX, 2 * DEPTH), bf16),
            pltpu.VMEM((PIX, DEPTH), f32),
            pltpu.VMEM((16 * requests, BLOCK), f32),
            dma((3, nb)),
            dma((3, nb)),
            dma((nr,)),
            dma((nr,)),
            dma((nx,)),
            dma((nx,)),
            dma(()),
            dma((2 * ITERS, nr)),
            dma((2 * ITERS, nr)),
            dma((ITERS, nx)),
            dma((ITERS, nx)),
            dma((2,)),
            dma((2,)),
        ],
        compiler_params=pltpu.CompilerParams(
            collective_id=0, has_side_effects=True, vmem_limit_bytes=48 * 1024 * 1024
        ),
        cost_estimate=pl.CostEstimate(flops=20_000_000_000, bytes_accessed=6_000_000, transcendentals=4_000_000),
        name="train",
    )(
        tile_corner.reshape(ITERS, 2 * tiles),
        own,
        migration[0],
        table,
        jnp.pad(jnp.transpose(slot).astype(f32), ((0, 0), (0, BLOCK - ITERS))),
        packed,
        depth_order.reshape(ITERS * tiles, 1, DEPTH),
        targets.reshape(ITERS * tiles, 3, PIX),
        params,
        first_moment,
        second_moment,
    )
    return new_params, new_first, new_second, pictures.reshape(ITERS, 1, tiles, 3, PIX)


def solution(mesh):
    return jax.shard_map(
        local,
        mesh=mesh,
        in_specs=(
            P(None, "row"),
            P(None, "row"),
            P(None, "row"),
            P(None, "rep", None),
            P(None, "rep", "row", None),
            P(None, "rep", "row", None),
            P(None, "rep", "row", None),
            P(None, "rep", "row", None),
            P(None, "rep", "row", None, None),
            P("row", None, None),
        ),
        out_specs=(
            P(None, "row"),
            P(None, "row"),
            P(None, "row"),
            P(None, "rep", "row", None, None),
        ),
        check_vma=False,
    )
```

time: 549 us -> 163 us (0.30); the launches traced: 539 us -> 160 us
  waiting for transfers between devices: 152 us -> 0 us
  Pallas kernels: 0 us -> 148 us
  other arithmetic: 106 us -> 1.02 us
  local copies, waits for them, and re-layouts: 99.7 us -> 10.2 us
  between operations: 55.4 us -> 0.7 us
  starting transfers between devices: 48 us -> 0 us
  matrix products: 42.3 us -> 0 us
  blocking collectives: 34.3 us -> 0 us
    pallas_call x0 -> x1, Pallas kernels: none -> 148 us  [local(): pl.pallas_call(functools.partial(kernel, nr, nx, nb, tiles), out_shape=(s...]
    all_to_all x5 -> x0, waiting for transfers between devices: 80.3 us -> none  [the longest x2 53.7 us: local(): lax.all_to_all(serve(projected, asked_blocks, blk_dev), 'row', split_axis...]
    psum x2 -> x0, waiting for transfers between devices: 65.6 us -> none  [local(): summed_grad = lax.psum(gradient, 'rep')]
    all_to_all x5 -> x0, starting transfers between devices: 44 us -> none  [the longest x2 20.8 us: local(): lax.all_to_all(serve(projected, asked_blocks, blk_dev), 'row', split_axis...]
    dot_general x24 -> x0, matrix products: 42.3 us -> none  [the longest x12 27 us: render(): jnp.einsum('cn,pn->cp', splat_rows[5:8], alphas * transmit, precision=lax...]
    all_to_all x1 -> x0, blocking collectives: 34.3 us -> none  [local(): lax.all_to_all(outgoing, 'row', split_axis=1, concat_axis=1, tiled=True)]
    gather x7 -> x0, local copies, waits for them, and re-layouts: 29.4 us -> none  [the longest x2 26.1 us: local(): sorted_rows = jnp.take_along_axis(tile_rows, orders[:, None, :], axis=2)]
    add_any x22 -> x0, other arithmetic: 26.4 us -> none  [the longest x2 8.99 us: project(): quat_z * quat_z]
  transfers between devices with their start and end apart: 9 -> 0, of which waited for: 6 -> 0; matrix products, arithmetic and copies ran while one was open for 7% -> 0% of each run, Pallas kernels for 0% -> 0%
where the time goes in v1:
time: 163 us; the launch traced here: 160 us
  Pallas kernels  148 us (91%)
  local copies, waits for them, and re-layouts  10.2 us (6%)
    pallas_call x1, Pallas kernels, local(): pl.pallas_call(functools.partial(kernel, nr, nx, nb, tiles), out_shape=(s...  148 us
    unnamed x25, local copies, waits for them, and re-layouts  9.52 us

profile of v1, /device:TPU:2, one launch (start us, length us, event | category | flops | bytes accessed | tf_op | source)
XLA Modules:
  0.0 160.4 jit_solution(13992421029709172536)
XLA Ops:
  0.6 0.5 broadcast.26
  1.2 0.2 copy-done
  1.3 0.7 reduce.3
  2.0 0.1 reshape_reshape.3
  2.2 0.5 copy-done.6
  2.7 0.1 reshape.44
  2.8 0.2 convert_reduce_fusion
  2.9 0.5 copy-done.8
  3.4 0.1 copy.39
  3.5 0.1 reshape.42.corner_ref
  3.6 0.6 copy-done.7
  4.2 0.1 convert_element_type.27
  4.3 0.1 copy.40
  4.4 0.1 copy.42
  4.5 0.1 copy.43
  4.7 0.5 copy-done.5
  5.3 0.7 copy-done.3
  6.0 1.2 copy-done.1
  7.2 1.2 copy-done.2
  8.4 148.4 %train.1 = (f32[59,4096]{1,0:T(8,128)S(1)}, f32[59,4096]{1,0:T(8,128)S(1)}, f32[59,4096]{1,0:T(8,128)S(1)}, f32[8,3,256]{2,1,0:T(4,128)S(1)}) custom-call(f32[2,8]{1,0:T(2,128)S(1)} %reshape.42.corner_ref, f32[2,11]{1,0:T(2,128)S(1)} %bitcast.10, s32[2,2]{1,0:T(2,128)S(1)} %bitcast.11, f32[8,128]{1,0:T(8,128)S(1)} %fusion.request_ref, ...), custom_call_target="tpu_custom_call" | custom-call | flops 20000000000 | bytes 6000000 | tf_op jit(solution)/shard_map/train/pallas_call | solution.py:699
  156.8 0.6 copy.47
  157.5 1.0 copy.51
  158.4 1.0 copy.52
  159.4 1.0 copy.53
  (21 shorter events, 0.3 us)
Async XLA Ops:
  0.6 0.7 copy-start
  2.0 0.7 copy-start.6
  2.8 0.7 copy-start.8
  3.5 0.7 copy-start.7
  4.5 0.7 copy-start.5
  4.5 0.7 copy-start.4
  5.3 0.7 copy-start.3
  5.9 1.2 copy-start.1
  7.2 1.2 copy-start.2

commit v2 on v1

--- a/solution.py
+++ b/solution.py
@@ -17,9 +17,10 @@
 DEPTH = 512
 NINE = 9
 CAP = 2
-STRIDE = 64
+STRIDE = 72
 PAIR = 24
-SENT = 18
+ROUND = 40
+UNROLL = 9
 MESH = pl.DeviceIdType.MESH
 f32 = jnp.float32
 bf16 = jnp.bfloat16
@@ -155,6 +156,8 @@
     shared,
     mig_send,
     mig_recv,
+    end_send,
+    end_recv,
     listing,
     listed_rows,
     picks,
@@ -182,6 +185,8 @@
     rep_rsem,
     mig_ssem,
     mig_rsem,
+    end_ssem,
+    end_rsem,
 ):
     me = lax.axis_index("row")
     rep = lax.axis_index("rep")
@@ -211,7 +216,7 @@
         pl.semaphore_signal(barrier, 1, device_id={"rep": lax.rem(rep + k, nx)}, device_id_type=MESH)
         return c
 
-    lax.fori_loop(1, nr, greet_row, 0)
+    lax.fori_loop(1, nr, greet_row, 0, unroll=UNROLL)
     lax.fori_loop(1, nx, greet_rep, 0)
 
     asked_now = jnp.full((nr, BLOCK), -1, jnp.int32)
@@ -268,6 +273,7 @@
     for part in range(2):
         lower[part * DEPTH : (part + 1) * DEPTH, :] = after
     listed_rows[...] = jnp.zeros_like(listed_rows)
+    request_grads[...] = jnp.zeros_like(request_grads)
 
     for a in range(3):
         lax.fori_loop(0, nb, lambda b, c: (load_copy(a, b).wait(), c)[1], 0)
@@ -279,7 +285,7 @@
         ref[pl.ds(r, nb, stride=STRIDE), :] = x
 
     def project(i):
-        cam = [own_ref[i, k] for k in range(11)]
+        cam = [own_ref[i, 0, k] for k in range(11)]
         affine = [cam[0:3], cam[3:6]]
         rows = functools.partial(row, p_s)
         scales, _, _, rotation = geometry(rows)
@@ -297,64 +303,85 @@
             colours.append(0.5 + total)
         return centre + list(conic) + colours + [sigmoid(rows(10))]
 
-    def put_slots(ref, values):
-        for s in range(CAP):
-            for c in range(NINE):
-                base = 8 * s + c if c < 8 else 16 + s
-                ref[pl.ds(base, nr, stride=PAIR), :] = values[s * nr : (s + 1) * nr, c * BLOCK : (c + 1) * BLOCK]
-
-    def get_slots(ref):
-        columns = []
+    def put_slot(ref, values):
         for c in range(NINE):
-            columns.append(
-                jnp.concatenate(
-                    [ref[pl.ds(8 * s + c if c < 8 else 16 + s, nr, stride=PAIR), :] for s in range(CAP)], axis=0
-                )
-            )
-        return jnp.concatenate(columns, axis=1)
-
-    def pair_rows(p):
-        return pl.ds(pl.multiple_of(PAIR * p, 8), SENT)
-
-    def slot_copy(send, recv, which, k, at):
+            ref[pl.ds(c, nr, stride=PAIR), :] = values[:, c * BLOCK : (c + 1) * BLOCK]
+
+    def get_slot(ref, components=range(NINE)):
+        return jnp.concatenate([ref[pl.ds(c, nr, stride=PAIR), :] for c in components], axis=1)
+
+    def nine_rows(p):
+        return pl.ds(pl.multiple_of(PAIR * p, 8), NINE)
+
+    def slot_copy(send, recv, which, s, k, at):
         to, _ = row_of(k)
         return pltpu.make_async_remote_copy(
-            src_ref=send.at[pair_rows(to), :],
-            dst_ref=recv.at[pair_rows(at), :],
-            send_sem=a2a_ssem.at[which, k],
-            recv_sem=a2a_rsem.at[which, k],
+            src_ref=send.at[s, nine_rows(to), :],
+            dst_ref=recv.at[s, nine_rows(at), :],
+            send_sem=a2a_ssem.at[CAP * which + s, k],
+            recv_sem=a2a_rsem.at[CAP * which + s, k],
             device_id={"row": to},
             device_id_type=MESH,
         )
 
-    def exchange(send, recv, which):
-        lax.fori_loop(1, nr, lambda k, c: (slot_copy(send, recv, which, k, me).start(), c)[1], 0)
-        own = pl.ds(pl.multiple_of(PAIR * me, 8), PAIR)
-        recv[own, :] = send[own, :]
-
-        def arrived(k, c):
-            copy = slot_copy(send, recv, which, k, row_of(k)[1])
-            copy.wait_recv()
-            copy.wait_send()
-            return c
-
-        lax.fori_loop(1, nr, arrived, 0)
-
-    def render(i, recv):
-        slot_lane = lax.broadcasted_iota(jnp.int32, (requests, CAP * nr), 1)
-        slot_lane = CAP * lax.rem(slot_lane, nr) + slot_lane // nr
-        take = jnp.where(column_ref[:, i : i + 1] == slot_lane.astype(f32), 1.0, 0.0).astype(bf16)
-        pieces = split3(get_slots(recv))
-        listed = dot(take, pieces[0]) + dot(take, pieces[1]) + dot(take, pieces[2])
-        for c in range(NINE):
-            listed_rows[pl.ds(c, requests, stride=16), :] = listed[:, BLOCK * c : BLOCK * (c + 1)]
+    def slot_start(send, recv, which, s):
+        lax.fori_loop(
+            1, nr, lambda k, c: (slot_copy(send, recv, which, s, k, me).start(), c)[1], 0, unroll=UNROLL
+        )
+        recv[s, nine_rows(me), :] = send[s, nine_rows(me), :]
+
+    def slot_arrive(send, recv, which, s):
+        lax.fori_loop(
+            1,
+            nr,
+            lambda k, c: (slot_copy(send, recv, which, s, k, row_of(k)[1]).wait_recv(), c)[1],
+            0,
+            unroll=UNROLL,
+        )
+
+    def slot_leave(send, recv, which):
+        for s in range(CAP):
+            lax.fori_loop(
+                1, nr, lambda k, c: (slot_copy(send, recv, which, s, k, me).wait_send(), c)[1], 0, unroll=UNROLL
+            )
+
+    def render(i, f_out, f_in, g_out, g_in):
+        def list_slot(s):
+            slot_lane = CAP * lax.broadcasted_iota(jnp.int32, (requests, nr), 1) + s
+            take = jnp.where(column_ref[:, i : i + 1] == slot_lane.astype(f32), 1.0, 0.0).astype(bf16)
+            slot_arrive(f_out, f_in, 2 * i, s)
+            pieces = split3(get_slot(f_in.at[s]))
+            listed = dot(take, pieces[0]) + dot(take, pieces[1]) + dot(take, pieces[2])
+            for c in range(NINE):
+                at = pl.ds(c, requests, stride=16)
+                fresh = listed[:, BLOCK * c : BLOCK * (c + 1)]
+                listed_rows[at, :] = fresh if s == 0 else listed_rows[at, :] + fresh
+
+        def return_slot(s):
+            by_request = jnp.concatenate(
+                [request_grads[pl.ds(c, requests, stride=16), :] for c in range(NINE)], axis=1
+            )
+            slot_line = CAP * lax.broadcasted_iota(jnp.int32, (nr, 3 * requests), 0) + s
+            back = jnp.where(slot_line.astype(f32) == request_ref[i : i + 1, 0 : 3 * requests], 1.0, 0.0).astype(bf16)
+            put_slot(g_out.at[s], dot(back, jnp.concatenate(split3(by_request), axis=0)))
+            slot_start(g_out, g_in, 2 * i + 1, s)
+
+        list_slot(0)
 
         def one_tile(t, carry):
+            @pl.when(t == 1)
+            def _():
+                list_slot(1)
+
+            @pl.when(t == tiles - 1)
+            def _():
+                return_slot(0)
+
             for j in range(LISTB):
                 listing[:, BLOCK * j : BLOCK * (j + 1)] = listed_rows[
                     pl.ds(pl.multiple_of(16 * (LISTB * t + j), 16), 16), :
                 ]
-            order = order_ref[pl.ds(i * tiles + t, 1), 0, :]
+            order = order_ref[i, 0, pl.ds(t, 1), :]
             pick = jnp.where(lax.broadcasted_iota(jnp.int32, (DEPTH, DEPTH), 0) == order, 1.0, 0.0).astype(bf16)
             picks[...] = pick
             parts = dot(jnp.concatenate(split3(listing[...]), axis=0), picks[...])
@@ -363,8 +390,8 @@
             conic_a, conic_b, conic_c = splats[2:3], splats[3:4], splats[4:5]
             opacity = splats[8:9]
             ticks = lax.broadcasted_iota(jnp.int32, (SIDE, DEPTH), 0).astype(f32)
-            gap_x = (corner_ref[i, 2 * t] + ticks + 0.5) - centre_x
-            gap_y = (corner_ref[i, 2 * t + 1] + ticks + 0.5) - centre_y
+            gap_x = (corner_ref[i, 0, t, 0] + ticks + 0.5) - centre_x
+            gap_y = (corner_ref[i, 0, t, 1] + ticks + 0.5) - centre_y
             along = -0.5 * conic_a * gap_x * gap_x
             cross = -conic_b * gap_y
             across = -0.5 * conic_c * gap_y * gap_y
@@ -389,8 +416,8 @@
             both = dot(jnp.concatenate([paint_high, paint_low], axis=0).astype(bf16), weight_high[...], NT)
             high_low = dot(jnp.concatenate([paint_high, paint_high], axis=0).astype(bf16), weight_low[...], NT)
             picture = both[0:8] + both[8:16] + high_low[0:8]
-            picture_ref[i * tiles + t] = picture[5:8]
-            residual = picture - jnp.concatenate([jnp.zeros((5, PIX), f32), target_ref[i * tiles + t]], axis=0)
+            picture_ref[i, 0, t] = picture[5:8]
+            residual = picture - jnp.concatenate([jnp.zeros((5, PIX), f32), target_ref[i, 0, t]], axis=0)
             res_high = residual.astype(bf16).astype(f32)
             res_low = residual - res_high
             pull = dot(
@@ -442,29 +469,46 @@
             return carry
 
         lax.fori_loop(0, tiles, one_tile, 0)
-
-    def step_up(r, gradient):
-        one = 0.9 * row(m_s, r) + 0.1 * gradient
-        two = 0.999 * row(v_s, r) + 0.001 * gradient * gradient
-        put_row(m_s, r, one)
-        put_row(v_s, r, two)
-        put_row(p_s, r, row(p_s, r) - learn_rate * one / (jnp.sqrt(two) + adam_epsilon))
-
-    def pull_back(i, shares):
-        rows = functools.partial(row, p_s)
-        scales, quats, inverse, rotation = geometry(rows)
-        cams = [[cam_smem[8 * x, 11 * i + k] for k in range(11)] for x in range(nx)]
+        return_slot(1)
+
+    def own_get(a, r):
+        return row(state[a], r)
+
+    def own_put(a, r, x):
+        put_row(state[a], r, x)
+
+    def step_up(get, put, r, gradient):
+        one = 0.9 * get(1, r) + 0.1 * gradient
+        two = 0.999 * get(2, r) + 0.001 * gradient * gradient
+        put(1, r, one)
+        put(2, r, two)
+        put(0, r, get(0, r) - learn_rate * one / (jnp.sqrt(two) + adam_epsilon))
+
+    def cameras(i):
+        return [[cam_smem[8 * x, 11 * i + k] for k in range(11)] for x in range(nx)]
+
+    def pull_colours(i, get, put, share):
+        opacity = sigmoid(get(0, 10))
+        fades = share(0, 8)
+        for x in range(1, nx):
+            fades = fades + share(x, 8)
+        step_up(get, put, 10, fades * opacity * (1.0 - opacity))
+        bases = [harmonics(*cam[8:11]) for cam in cameras(i)]
+        for k in range(3):
+            felt = [share(x, 5 + k) for x in range(nx)]
+            for j in range(16):
+                total = bases[0][j] * felt[0]
+                for x in range(1, nx):
+                    total = total + bases[x][j] * felt[x]
+                step_up(get, put, 11 + 3 * j + k, total)
+
+    def pull_shapes(i, get, put, share):
+        scales, quats, inverse, rotation = geometry(lambda r: get(0, r))
         turn = None
-        for x in range(nx):
-            cam = cams[x]
+        for x, cam in enumerate(cameras(i)):
             affine = [cam[0:3], cam[3:6]]
-
-            def share(c):
-                at = (x * NINE + c) * nb
-                return shares[at : at + nb, :]
-
             spread, (con_a, con_b, con_c) = conic_of(affine, scales, rotation)
-            g_a, g_b, g_c = share(2), 0.5 * share(3), share(4)
+            g_a, g_b, g_c = share(x, 2), 0.5 * share(x, 3), share(x, 4)
             left_a, left_b = g_a * con_a + g_b * con_b, g_a * con_b + g_b * con_c
             right_a, right_b = g_b * con_a + g_c * con_b, g_b * con_b + g_c * con_c
             n_xx = -2.0 * (con_a * left_a + con_b * right_a)
@@ -479,15 +523,13 @@
                 [(affine[0][j] * felt[0][k] + affine[1][j] * felt[1][k]) * scales[k] for k in range(3)]
                 for j in range(3)
             ]
-            moved = [affine[0][j] * share(0) + affine[1][j] * share(1) for j in range(3)]
-            fade = share(8)
+            moved = [affine[0][j] * share(x, 0) + affine[1][j] * share(x, 1) for j in range(3)]
             if turn is None:
-                stretches, turn, moves, fades = stretch, twist, moved, fade
+                stretches, turn, moves = stretch, twist, moved
             else:
                 stretches = [u + v for u, v in zip(stretches, stretch)]
                 turn = [[u + v for u, v in zip(a, b)] for a, b in zip(turn, twist)]
                 moves = [u + v for u, v in zip(moves, moved)]
-                fades = fades + fade
         w, x, y, z = quats
         d = turn
         unit = [
@@ -515,33 +557,85 @@
             ),
         ]
         inner = unit[0] * w + unit[1] * x + unit[2] * y + unit[3] * z
-        opacity = sigmoid(rows(10))
         for k in range(3):
-            step_up(k, moves[k])
+            step_up(get, put, k, moves[k])
         for k in range(3):
-            step_up(3 + k, stretches[k])
+            step_up(get, put, 3 + k, stretches[k])
         for k in range(4):
-            step_up(6 + k, (unit[k] - quats[k] * inner) * inverse)
-        step_up(10, fades * opacity * (1.0 - opacity))
-        bases = [harmonics(*cam[8:11]) for cam in cams]
-        for k in range(3):
-            felt = [shares[(x * NINE + 5 + k) * nb : (x * NINE + 6 + k) * nb, :] for x in range(nx)]
-            for j in range(16):
-                total = bases[0][j] * felt[0]
-                for x in range(1, nx):
-                    total = total + bases[x][j] * felt[x]
-                step_up(11 + 3 * j + k, total)
-
-    def share_copy(i, k, at):
-        size = NINE * nb
+            step_up(get, put, 6 + k, (unit[k] - quats[k] * inner) * inverse)
+
+    parts_of = ((5, 4), (0, 5))
+
+    def share_copy(i, part, k, at):
+        first, count = parts_of[part]
+
+        def rows_at(x):
+            return pl.ds(pl.multiple_of((NINE * x + first) * nb, 8), count * nb)
+
         return pltpu.make_async_remote_copy(
-            src_ref=shared.at[i, pl.ds(pl.multiple_of(size * rep, 8), size), :],
-            dst_ref=shared.at[i, pl.ds(pl.multiple_of(size * at, 8), size), :],
-            send_sem=rep_ssem.at[i, k],
-            recv_sem=rep_rsem.at[i, k],
+            src_ref=shared.at[i, rows_at(rep), :],
+            dst_ref=shared.at[i, rows_at(at), :],
+            send_sem=rep_ssem.at[2 * i + part, k],
+            recv_sem=rep_rsem.at[2 * i + part, k],
             device_id={"rep": lax.rem(rep + k, nx)},
             device_id_type=MESH,
         )
+
+    hand = MIGH * 3 * STRIDE
+    round_rows = MIGH * ROUND
+
+    def neighbour(side):
+        return {"row": lax.rem(me + (nr - 1 if side == 0 else 1), nr)}
+
+    def hand_copy(side):
+        return pltpu.make_async_remote_copy(
+            src_ref=mig_send.at[pl.ds(side * hand, hand), :],
+            dst_ref=mig_recv.at[pl.ds((1 - side) * hand, hand), :],
+            send_sem=mig_ssem.at[side],
+            recv_sem=mig_rsem.at[side],
+            device_id=neighbour(side),
+            device_id_type=MESH,
+        )
+
+    def end_copy(side):
+        return pltpu.make_async_remote_copy(
+            src_ref=end_send.at[pl.ds(side * round_rows, round_rows), :],
+            dst_ref=end_recv.at[pl.ds((1 - side) * round_rows, round_rows), :],
+            send_sem=end_ssem.at[side],
+            recv_sem=end_rsem.at[side],
+            device_id=neighbour(side),
+            device_id_type=MESH,
+        )
+
+    def hand_over():
+        for side in range(2):
+            for j in range(MIGH):
+                leaving = jnp.full((STRIDE, BLOCK), migration_ref[0, side, j], jnp.int32)
+                for a in range(3):
+                    at = side * hand + (3 * j + a) * STRIDE
+                    chosen = state[a][0:STRIDE, :]
+                    for b in range(1, nb):
+                        chosen = jnp.where(leaving == b, state[a][STRIDE * b : STRIDE * (b + 1), :], chosen)
+                    mig_send[at : at + STRIDE, :] = chosen
+            hand_copy(side).start()
+
+    def hand_gradients(share):
+        count = 2 * MIGH
+        line = lax.broadcasted_iota(jnp.int32, (8, 3 * nb), 0)
+        block_lane = lax.rem(lax.broadcasted_iota(jnp.int32, (8, 3 * nb), 1), nb)
+        mine = jnp.full((8, 3 * nb), -1, jnp.int32)
+        for side in range(2):
+            for j in range(MIGH):
+                mine = jnp.where(line == MIGH * side + j, migration_ref[0, side, j], mine)
+        choose = jnp.where(mine == block_lane, 1.0, 0.0)
+        choose = jnp.concatenate([choose, jnp.zeros_like(choose)], axis=0).astype(bf16)
+        for x in range(nx):
+            values = jnp.concatenate([share(x, c) for c in range(NINE)], axis=1)
+            chosen = dot(choose, jnp.concatenate(split3(values), axis=0))
+            for c in range(NINE):
+                end_send[pl.ds(NINE * x + c, count, stride=ROUND), :] = chosen[0:count, BLOCK * c : BLOCK * (c + 1)]
+        for side in range(2):
+            end_copy(side).start()
 
     asked_columns = asked_lines = None
     for i in range(ITERS):
@@ -570,29 +664,35 @@
             ],
             axis=0,
         ).astype(bf16)
-        put_slots(f_send.at[i], dot(serve, jnp.concatenate(split3(projected), axis=0)))
-        exchange(f_send.at[i], f_recv.at[i], 2 * i)
-        render(i, f_recv.at[i])
-        by_request = jnp.concatenate([request_grads[pl.ds(c, requests, stride=16), :] for c in range(NINE)], axis=1)
-        slot_line = lax.broadcasted_iota(jnp.int32, (CAP * nr, 3 * requests), 0)
-        slot_line = CAP * lax.rem(slot_line, nr) + slot_line // nr
-        back = jnp.where(slot_line.astype(f32) == request_ref[i : i + 1, 0 : 3 * requests], 1.0, 0.0).astype(bf16)
-        put_slots(g_send.at[i], dot(back, jnp.concatenate(split3(by_request), axis=0)))
-        exchange(g_send.at[i], g_recv.at[i], 2 * i + 1)
-        wanted = jnp.concatenate(
-            [asked_lines[CAP * i + s : CAP * i + s + 1, 0:nr] for s in range(CAP)], axis=1
-        )
-        gather = jnp.where(
-            lax.broadcasted_iota(jnp.int32, (nb, CAP * nr), 0).astype(f32) == wanted, 1.0, 0.0
-        ).astype(bf16)
-        pieces = split3(get_slots(g_recv.at[i]))
-        summed = dot(gather, pieces[0]) + dot(gather, pieces[1]) + dot(gather, pieces[2])
-        for c in range(NINE):
-            shared[i, pl.ds(pl.multiple_of(NINE * nb * rep + nb * c, 8), nb), :] = summed[
-                :, BLOCK * c : BLOCK * (c + 1)
-            ]
-        for k in range(1, nx):
-            share_copy(i, k, rep).start()
+        slots = jnp.concatenate(split3(projected), axis=0)
+        for s in range(CAP):
+            put_slot(f_send.at[i, s], dot(serve[s * nr : (s + 1) * nr], slots))
+            slot_start(f_send.at[i], f_recv.at[i], 2 * i, s)
+        render(i, f_send.at[i], f_recv.at[i], g_send.at[i], g_recv.at[i])
+        slot_leave(f_send.at[i], f_recv.at[i], 2 * i)
+        block_line = lax.broadcasted_iota(jnp.int32, (nb, nr), 0).astype(f32)
+        gathers = [
+            jnp.where(block_line == asked_lines[CAP * i + s : CAP * i + s + 1, 0:nr], 1.0, 0.0).astype(bf16)
+            for s in range(CAP)
+        ]
+
+        def sum_slot(s, first, count):
+            pieces = split3(get_slot(g_recv.at[i, s], range(first, first + count)))
+            return dot(gathers[s], pieces[0]) + dot(gathers[s], pieces[1]) + dot(gathers[s], pieces[2])
+
+        slot_arrive(g_send.at[i], g_recv.at[i], 2 * i + 1, 0)
+        sums = [sum_slot(0, *parts_of[part]) for part in range(2)]
+        slot_arrive(g_send.at[i], g_recv.at[i], 2 * i + 1, 1)
+        for part in range(2):
+            first, count = parts_of[part]
+            summed = sums[part] + sum_slot(1, first, count)
+            for c in range(count):
+                shared[i, pl.ds(pl.multiple_of((NINE * rep + first + c) * nb, 8), nb), :] = summed[
+                    :, BLOCK * c : BLOCK * (c + 1)
+                ]
+            for k in range(1, nx):
+                share_copy(i, part, k, rep).start()
+        slot_leave(g_send.at[i], g_recv.at[i], 2 * i + 1)
         if i == 0:
             for k in range(1, nx):
                 copy = cam_copy(k, lax.rem(rep + nx - k, nx))
@@ -601,38 +701,43 @@
             table = pltpu.make_async_copy(cam_recv, cam_smem, cam_sem)
             table.start()
             table.wait()
-        for k in range(1, nx):
-            copy = share_copy(i, k, lax.rem(rep + nx - k, nx))
-            copy.wait_recv()
-            copy.wait_send()
-        pull_back(i, shared.at[i])
-
-    hand = MIGH * 3 * STRIDE
-
-    def hand_copy(side):
-        to = lax.rem(me + (nr - 1 if side == 0 else 1), nr)
-        return pltpu.make_async_remote_copy(
-            src_ref=mig_send.at[pl.ds(side * hand, hand), :],
-            dst_ref=mig_recv.at[pl.ds((1 - side) * hand, hand), :],
-            send_sem=mig_ssem.at[side],
-            recv_sem=mig_rsem.at[side],
-            device_id={"row": to},
-            device_id_type=MESH,
-        )
-
-    for side in range(2):
-        for j in range(MIGH):
-            leaving = jnp.full((STRIDE, BLOCK), migration_ref[side, j], jnp.int32)
-            for a in range(3):
-                at = side * hand + (3 * j + a) * STRIDE
-                chosen = state[a][0:STRIDE, :]
-                for b in range(1, nb):
-                    chosen = jnp.where(leaving == b, state[a][STRIDE * b : STRIDE * (b + 1), :], chosen)
-                mig_send[at : at + STRIDE, :] = chosen
-        hand_copy(side).start()
+
+        def own_share(x, c):
+            at = (x * NINE + c) * nb
+            return shared[i, at : at + nb, :]
+
+        def arrive_share(part):
+            for k in range(1, nx):
+                copy = share_copy(i, part, k, lax.rem(rep + nx - k, nx))
+                copy.wait_recv()
+                copy.wait_send()
+
+        arrive_share(0)
+        pull_colours(i, own_get, own_put, own_share)
+        arrive_share(1)
+        if i == ITERS - 1:
+            hand_gradients(own_share)
+        pull_shapes(i, own_get, own_put, own_share)
+        if i == ITERS - 2:
+            hand_over()
+
     for side in range(2):
         hand_copy(side).wait_recv()
         hand_copy(side).wait_send()
+        end_copy(side).wait_recv()
+        end_copy(side).wait_send()
+
+    def come_get(a, r):
+        return mig_recv[pl.ds(a * STRIDE + r, 2 * MIGH, stride=3 * STRIDE), :]
+
+    def come_put(a, r, x):
+        mig_recv[pl.ds(a * STRIDE + r, 2 * MIGH, stride=3 * STRIDE), :] = x
+
+    def come_share(x, c):
+        return end_recv[pl.ds(NINE * x + c, 2 * MIGH, stride=ROUND), :]
+
+    pull_colours(ITERS - 1, come_get, come_put, come_share)
+    pull_shapes(ITERS - 1, come_get, come_put, come_share)
 
     def settle(b, carry):
         for a in range(3):
@@ -641,7 +746,7 @@
             for side in range(2):
                 for j in range(MIGH):
                     source = side * hand + (3 * j + a) * STRIDE
-                    here = jnp.full((STRIDE, BLOCK), migration_ref[side, j], jnp.int32) == b
+                    here = jnp.full((STRIDE, BLOCK), migration_ref[0, side, j], jnp.int32) == b
                     block = jnp.where(here, mig_recv[source : source + STRIDE, :], block)
             state[a][at, :] = block
             store_copy(a, b).start()
@@ -678,7 +783,8 @@
     block = tile_block.reshape(ITERS, requests)
     position = jnp.arange(requests, dtype=jnp.int32)
     same = (owner[:, :, None] == owner[:, None, :]) & (position[None, :] < position[:, None])
-    slot = owner * CAP + jnp.sum(same.astype(jnp.int32), axis=2)
+    later = jnp.any(same, axis=2) | (position >= requests - LISTB)[None, :]
+    slot = owner * CAP + later.astype(jnp.int32)
     wide = jnp.concatenate([slot, slot, slot], axis=1).astype(f32)
     table = jnp.concatenate(
         [
@@ -698,7 +804,7 @@
     dma = pltpu.SemaphoreType.DMA
     new_params, new_first, new_second, pictures = pl.pallas_call(
         functools.partial(kernel, nr, nx, nb, tiles),
-        out_shape=(size, size, size, jax.ShapeDtypeStruct((ITERS * tiles, 3, PIX), f32)),
+        out_shape=(size, size, size, jax.ShapeDtypeStruct((ITERS, 1, tiles, 3, PIX), f32)),
         in_specs=[smem] * 3 + [vmem] * 5 + [hbm] * 3,
         out_specs=(hbm, hbm, hbm, vmem),
         scratch_shapes=[
@@ -709,13 +815,15 @@
             pltpu.VMEM((8 * nr, BLOCK), jnp.int32),
             pltpu.VMEM((8 * nx, BLOCK), f32),
             pltpu.SMEM((8 * nx, BLOCK), f32),
-            pltpu.VMEM((ITERS, PAIR * nr, BLOCK), f32),
-            pltpu.VMEM((ITERS, PAIR * nr, BLOCK), f32),
-            pltpu.VMEM((ITERS, PAIR * nr, BLOCK), f32),
-            pltpu.VMEM((ITERS, PAIR * nr, BLOCK), f32),
+            pltpu.VMEM((ITERS, CAP, PAIR * nr, BLOCK), f32),
+            pltpu.VMEM((ITERS, CAP, PAIR * nr, BLOCK), f32),
+            pltpu.VMEM((ITERS, CAP, PAIR * nr, BLOCK), f32),
+            pltpu.VMEM((ITERS, CAP, PAIR * nr, BLOCK), f32),
             pltpu.VMEM((ITERS, nx * NINE * nb, BLOCK), f32),
             pltpu.VMEM((2 * MIGH * 3 * STRIDE, BLOCK), f32),
             pltpu.VMEM((2 * MIGH * 3 * STRIDE, BLOCK), f32),
+            pltpu.VMEM((2 * MIGH * ROUND, BLOCK), f32),
+            pltpu.VMEM((2 * MIGH * ROUND, BLOCK), f32),
             pltpu.VMEM((16, DEPTH), f32),
             pltpu.VMEM((16 * requests, BLOCK), f32),
             pltpu.VMEM((DEPTH, DEPTH), bf16),
@@ -737,10 +845,12 @@
             dma((nx,)),
             dma((nx,)),
             dma(()),
-            dma((2 * ITERS, nr)),
-            dma((2 * ITERS, nr)),
-            dma((ITERS, nx)),
-            dma((ITERS, nx)),
+            dma((2 * ITERS * CAP, nr)),
+            dma((2 * ITERS * CAP, nr)),
+            dma((2 * ITERS, nx)),
+            dma((2 * ITERS, nx)),
+            dma((2,)),
+            dma((2,)),
             dma((2,)),
             dma((2,)),
         ],
@@ -750,19 +860,19 @@
         cost_estimate=pl.CostEstimate(flops=20_000_000_000, bytes_accessed=6_000_000, transcendentals=4_000_000),
         name="train",
     )(
-        tile_corner.reshape(ITERS, 2 * tiles),
-        own,
-        migration[0],
+        tile_corner,
+        camera,
+        migration,
         table,
         jnp.pad(jnp.transpose(slot).astype(f32), ((0, 0), (0, BLOCK - ITERS))),
         packed,
-        depth_order.reshape(ITERS * tiles, 1, DEPTH),
-        targets.reshape(ITERS * tiles, 3, PIX),
+        depth_order,
+        targets,
         params,
         first_moment,
         second_moment,
     )
-    return new_params, new_first, new_second, pictures.reshape(ITERS, 1, tiles, 3, PIX)
+    return new_params, new_first, new_second, pictures
 
 
 def solution(mesh):

time: 163 us -> 149 us (0.914)
  Pallas kernels: 148 us -> 135 us
    pallas_call x1, Pallas kernels: 148 us -> 135 us  [local(): pl.pallas_call(functools.partial(kernel, nr, nx, nb, tiles), out_shape=(s...]
    unnamed x25 -> x24, local copies, waits for them, and re-layouts: 9.52 us -> 8.43 us
where the time goes in v2:
time: 149 us; the launch traced here: 147 us
  Pallas kernels  135 us (91%)
  local copies, waits for them, and re-layouts  9.64 us (6%)
    pallas_call x1, Pallas kernels, local(): pl.pallas_call(functools.partial(kernel, nr, nx, nb, tiles), out_shape=(s...  135 us
    unnamed x24, local copies, waits for them, and re-layouts  8.43 us

profile of v2, /device:TPU:2, one launch (start us, length us, event | category | flops | bytes accessed | tf_op | source)
XLA Modules:
  0.0 146.7 jit_solution(13612291040323017793)
XLA Ops:
  0.6 0.5 broadcast.35
  1.2 0.2 copy-done
  1.3 0.7 reduce.3
  2.0 0.1 reshape_reshape.3
  2.2 0.6 copy-done.6
  2.7 0.1 reshape.31
  2.8 0.2 and_reduce_fusion
  3.0 0.1 copy.36
  3.1 0.4 copy-done.8
  3.5 0.1 copy.40.corner_ref
  3.6 0.1 copy-done.7
  3.7 0.1 convert_element_type.27
  3.8 0.1 copy.34
  4.0 0.1 copy.37
  4.1 0.1 add_convert_fusion
  4.2 0.5 copy-done.5
  4.7 0.7 copy-done.3
  5.4 1.2 copy-done.1
  6.7 1.2 copy-done.2
  7.9 135.3 %train.1 = (f32[59,4096]{1,0:T(8,128)S(1)}, f32[59,4096]{1,0:T(8,128)S(1)}, f32[59,4096]{1,0:T(8,128)S(1)}, f32[2,1,4,3,256]{4,3,2,1,0:T(4,128)S(1)}) custom-call(f32[2,1,4,2]{3,2,1,0:T(4,128)S(1)} %copy.40.corner_ref, f32[2,1,11]{2,1,0:T(1,128)S(1)} %copy-done, s32[1,2,2]{2,1,0:T(2,128)S(1)} %copy-done.4, f32[8,128]{1,0:T(8,128)S(1)} %fusion.request_ref, ...), custom_call_target="tpu_custom_call" | custom-call | flops 20000000000 | bytes 6000000 | tf_op jit(solution)/shard_map/train/pallas_call | solution.py:805
  143.2 0.6 copy.42
  143.8 1.0 copy.46
  144.8 1.0 copy.47
  145.7 1.0 copy.48
  (20 shorter events, 0.3 us)
Async XLA Ops:
  0.6 0.7 copy-start
  2.1 0.7 copy-start.6
  2.8 0.7 copy-start.8
  3.0 0.7 copy-start.7
  4.0 0.7 copy-start.5
  4.7 0.7 copy-start.3
  4.7 0.7 copy-start.4
  5.4 1.2 copy-start.1
  6.7 1.2 copy-start.2

commit v3 on v2

--- a/solution.py
+++ b/solution.py
@@ -131,8 +131,6 @@
     own_ref,
     migration_ref,
     request_ref,
-    column_ref,
-    camera_ref,
     order_ref,
     target_ref,
     p_hbm,
@@ -231,7 +229,12 @@
             )
             asked_now = jnp.where(lane == CAP * i + s, column.astype(jnp.int32) - 1, asked_now)
     ask_send[pl.ds(0, nr, stride=8), :] = asked_now
-    cam_recv[pl.ds(pl.multiple_of(8 * rep, 8), 1), :] = camera_ref[...]
+    wide_lane = lax.broadcasted_iota(jnp.int32, (1, BLOCK), 1)
+    views = jnp.zeros((1, BLOCK), f32)
+    for i in range(ITERS):
+        for k in range(11):
+            views = jnp.where(wide_lane == 11 * i + k, own_ref[i, 0, k], views)
+    cam_recv[pl.ds(pl.multiple_of(8 * rep, 8), 1), :] = views
 
     pl.semaphore_wait(barrier, nr + nx - 2)
 
@@ -264,6 +267,10 @@
         cam_copy(k, rep).start()
     own_ask = pl.ds(pl.multiple_of(8 * me, 8), 8)
     ask_recv[own_ask, :] = ask_send[own_ask, :]
+
+    slot_columns = jnp.transpose(
+        jnp.concatenate([request_ref[...], jnp.zeros((BLOCK - 8, BLOCK), f32)], axis=0)
+    )[0:requests, :]
 
     square = lax.broadcasted_iota(jnp.int32, (DEPTH, DEPTH), 0), lax.broadcasted_iota(jnp.int32, (DEPTH, DEPTH), 1)
     before = jnp.where(square[0] < square[1], 1.0, 0.0).astype(bf16)
@@ -348,7 +355,7 @@
     def render(i, f_out, f_in, g_out, g_in):
         def list_slot(s):
             slot_lane = CAP * lax.broadcasted_iota(jnp.int32, (requests, nr), 1) + s
-            take = jnp.where(column_ref[:, i : i + 1] == slot_lane.astype(f32), 1.0, 0.0).astype(bf16)
+            take = jnp.where(slot_columns[:, i : i + 1] == slot_lane.astype(f32), 1.0, 0.0).astype(bf16)
             slot_arrive(f_out, f_in, 2 * i, s)
             pieces = split3(get_slot(f_in.at[s]))
             listed = dot(take, pieces[0]) + dot(take, pieces[1]) + dot(take, pieces[2])
@@ -794,8 +801,6 @@
         ],
         axis=0,
     )
-    own = camera.reshape(ITERS, 11)
-    packed = jnp.pad(own.reshape(1, ITERS * 11), ((0, 0), (0, BLOCK - ITERS * 11)))
 
     vmem = pl.BlockSpec(memory_space=pltpu.VMEM)
     smem = pl.BlockSpec(memory_space=pltpu.SMEM)
@@ -805,7 +810,7 @@
     new_params, new_first, new_second, pictures = pl.pallas_call(
         functools.partial(kernel, nr, nx, nb, tiles),
         out_shape=(size, size, size, jax.ShapeDtypeStruct((ITERS, 1, tiles, 3, PIX), f32)),
-        in_specs=[smem] * 3 + [vmem] * 5 + [hbm] * 3,
+        in_specs=[smem] * 3 + [vmem] * 3 + [hbm] * 3,
         out_specs=(hbm, hbm, hbm, vmem),
         scratch_shapes=[
             pltpu.VMEM((STRIDE * nb, BLOCK), f32),
@@ -864,8 +869,6 @@
         camera,
         migration,
         table,
-        jnp.pad(jnp.transpose(slot).astype(f32), ((0, 0), (0, BLOCK - ITERS))),
-        packed,
         depth_order,
         targets,
         params,

time: 149 us -> 147 us (0.987)
    unnamed x24 -> x19, local copies, waits for them, and re-layouts: 8.43 us -> 6.85 us
where the time goes in v3:
time: 147 us; the launch traced here: 145 us
  Pallas kernels  135 us (92%)
  local copies, waits for them, and re-layouts  8.4 us (6%)
    pallas_call x1, Pallas kernels, local(): pl.pallas_call(functools.partial(kernel, nr, nx, nb, tiles), out_shape=(s...  135 us
    unnamed x19, local copies, waits for them, and re-layouts  6.85 us

profile of v3, /device:TPU:2, one launch (start us, length us, event | category | flops | bytes accessed | tf_op | source)
XLA Modules:
  0.0 144.7 jit_solution(15070269119478464437)
XLA Ops:
  0.6 0.0 copy-start.5
  0.7 0.1 pad.12.clone
  0.7 0.8 reshape.31
  1.5 0.2 and_reduce_fusion
  1.7 0.0 copy-start.6
  1.7 0.1 add_convert_fusion
  1.8 0.8 copy.17.corner_ref
  2.6 0.0 copy-done.6
  2.6 0.1 convert_element_type.17
  2.7 0.1 fusion.request_ref
  2.7 0.0 copy-done.5
  2.7 0.0 copy-start.2
  2.7 0.0 copy-start.3
  2.7 0.0 copy-start.4
  2.8 0.7 copy-done.2
  3.5 0.0 copy-done.3
  3.5 0.0 copy-done.4
  3.5 1.2 copy-done
  4.7 1.2 copy-done.1
  5.9 135.2 %train.1 = (f32[59,4096]{1,0:T(8,128)S(1)}, f32[59,4096]{1,0:T(8,128)S(1)}, f32[59,4096]{1,0:T(8,128)S(1)}, f32[2,1,4,3,256]{4,3,2,1,0:T(4,128)S(1)}) custom-call(f32[2,1,4,2]{3,2,1,0:T(4,128)S(1)} %copy.17.corner_ref, f32[2,1,11]{2,1,0:T(1,128)S(1)} %copy-done.3, s32[1,2,2]{2,1,0:T(2,128)S(1)} %copy-done.4, f32[8,128]{1,0:T(8,128)S(1)} %fusion.request_ref, ...), custom_call_target="tpu_custom_call" | custom-call | flops 20000000000 | bytes 6000000 | tf_op jit(solution)/shard_map/train/pallas_call | solution.py:810
  141.2 0.6 copy.19
  141.8 1.0 copy.23
  142.8 1.0 copy.24
  143.7 1.0 copy.25
  (8 shorter events, 0.0 us)
Async XLA Ops:
  0.6 2.1 %copy-start.5 = (f32[2,1,4,3,256]{4,2,3,1,0:T(4,128)S(1)}, f32[2,1,4,3,256]{4,2,3,1,0:T(4,128)}, u32[]{:S(2)}) copy-start(f32[2,1,4,3,256]{4,2,3,1,0:T(4,128)} %param.18) | copy-start | bytes 73732
  1.7 0.9 copy-start.6
  2.7 0.7 copy-start.2
  2.7 0.7 copy-start.3
  2.7 0.7 copy-start.4
  3.5 1.2 copy-start
  4.7 1.2 copy-start.1
